TPU v7x, 32 devices: a whole 2x2x4 slice. The times are simulated.
32 devices in a mesh: exp: 8 (over y, x, core), tp: 4 (over z).
Axes of the slice: x: 2, y: 2, z: 4, core: 2. Of those that a mesh axis runs over, the one named last changes fastest.
Arguments:
- tokens: bfloat16 [4096, 1536], P('exp'), may hold values from -6 to 6
- attn_gain: float32 [1536], replicated, may hold values from 0.1 to 1.9
- moe_gain: float32 [1536], replicated, may hold values from 0.1 to 1.9
- w_qkv: bfloat16 [1536, 2560], P(None, 'tp'), may hold values from -0.15625 to 0.15625
- w_out: bfloat16 [1536, 1536], P('tp'), may hold values from -0.625 to 0.625
- w_router: bfloat16 [1536, 16], replicated, may hold values from -0.078125 to 0.078125
- w_gate: bfloat16 [16, 1536, 512], P('exp', None, 'tp'), may hold values from -0.15625 to 0.15625
- w_up: bfloat16 [16, 1536, 512], P('exp', None, 'tp'), may hold values from -0.15625 to 0.15625
- w_down: bfloat16 [16, 512, 1536], P('exp', 'tp'), may hold values from -1.5 to 1.5
- qkv_down: bfloat16 [1536, 128], replicated, may hold values from -0.15625 to 0.15625
- qkv_up: bfloat16 [128, 2560], P(None, 'tp'), may hold values from -1.5 to 1.5
- out_down: bfloat16 [1536, 128], P('tp'), may hold values from -0.625 to 0.625
- out_up: bfloat16 [128, 1536], replicated, may hold values from -1.5 to 1.5
- lengths: int32 [8, 4], P('exp'), may hold values from 1 to 341, 448 in all within a row
- adapter_index: int32 [8, 4], P('exp'), may hold values from 0 to 7
- loss_mask: int32 [4096], P('exp'), may hold values 0 or 1
- routes: int32 [4096, 8], P('exp'), may hold values from 0 to 15, all different within a row; in each aligned block of 512 rows (0 to 511, 512 to 1023, ...) at most 512 rows name the same one
- upstream: bfloat16 [4096, 1536], P('exp'), may hold values from -6 to 6
Outputs:
- output: bfloat16 [4096, 1536], P('exp')
- input_grad: bfloat16 [4096, 1536], P('exp')
- grad_qkv_down: float32 [1536, 128], replicated
- grad_qkv_up: float32 [128, 2560], P(None, 'tp')
- grad_out_down: float32 [1536, 128], P('tp')
- grad_out_up: float32 [128, 1536], replicated
Inputs may be any that keep to these rules, and one draw needn't show every extreme that they name: `routes`: each row names 8 different experts; in each aligned block of 512 rows (the rows of one device) no expert is named more than 512 times, a bound that some block reaches. Each device's 4 lengths sum to 448, and the largest is exactly 341.
All inputs are finite; a program needn't handle non-finite values. No bound on the sum of `loss_mask` on one device may be relied on, other than what follows from the above.
Results may differ from a plain program's by a relative error of at most 0.025.
Values may be sent and summed in bfloat16 or wider, within the bound.
No kernel may reach another device: no remote copies, remote signals or barrier semaphores. Data moves between devices by JAX's collectives and lax.ppermute only.
A program may use at most 256 MiB of HBM per device.

v0:
```python
import math

import jax
import jax.numpy as jnp
from jax import lax
from jax.sharding import PartitionSpec as P

D = 1536
HEADS = 24
KV_HEADS = 8
HD = 64
TOP = 8
RANK = 16
ADAPTERS = 8
EXP_DEV = 2
DOCS = 4
TOK_DEV = 512


EPS = 1e-06
ROPE_BASE = 10000.0
LOCAL_FORMS = ("secd,edf->secf", "secf,efd->secd", "secd,efd->secf", "secf,edf->secd")


def product(left_m, right_m):
    return jnp.dot(left_m, right_m, preferred_element_type=jnp.float32)


def contract(einsum_form, left_m, right_m):
    return jnp.einsum(einsum_form, left_m, right_m, preferred_element_type=jnp.float32)


def rms_norm(vectors, gain_vec):
    inv_root = lax.rsqrt(jnp.mean(vectors * vectors, axis=-1, keepdims=True) + EPS)
    return vectors * inv_root * gain_vec


def rms_norm_back(vectors, gain_vec, upstream_grad):
    inv_root = lax.rsqrt(jnp.mean(vectors * vectors, axis=-1, keepdims=True) + EPS)
    weighted = upstream_grad * gain_vec
    return inv_root * weighted - vectors * (inv_root * inv_root * inv_root) * jnp.mean(
        vectors * weighted, axis=-1, keepdims=True
    )


def layout(length_row, index_row):
    places = jnp.arange(TOK_DEV, dtype=jnp.int32)
    doc_ends = jnp.cumsum(length_row)
    doc_starts = doc_ends - length_row
    member = (places[:, None] >= doc_starts[None, :]) & (places[:, None] < doc_ends[None, :])
    occupied = jnp.any(member, axis=1)
    position = jnp.sum(jnp.where(member, places[:, None] - doc_starts[None, :], 0), axis=1)
    owner_doc = jnp.sum(jnp.where(member, jnp.arange(DOCS, dtype=jnp.int32)[None, :], 0), axis=1)
    doc_ident = jnp.where(occupied, owner_doc, DOCS + places)
    chosen = jnp.sum(jnp.where(member, index_row[None, :], 0), axis=1)
    adapter_pick = occupied[:, None] & (
        chosen[:, None] == jnp.arange(ADAPTERS, dtype=jnp.int32)[None, :]
    )
    rank_mask = jnp.repeat(jnp.where(adapter_pick, 1.0, 0.0).astype(jnp.float32), RANK, axis=1)
    return (occupied, position, doc_ident, rank_mask)


def angles(position):
    half_width = HD // 2
    frequency = jnp.exp(-math.log(ROPE_BASE) * jnp.arange(half_width, dtype=jnp.float32) * 2.0 / HD)
    turned = position.astype(jnp.float32)[:, None] * frequency[None, :]
    return (jnp.cos(turned), jnp.sin(turned))


def rotate(vectors, cosine, sine_table):
    half_width = vectors.shape[-1] // 2
    front_half = vectors[..., :half_width]
    back_half = vectors[..., half_width:]
    return jnp.concatenate(
        [
            front_half * cosine - back_half * sine_table,
            back_half * cosine + front_half * sine_table,
        ],
        axis=-1,
    )


def tables(route_rows, experts, capacity):
    flat_route = route_rows.reshape(-1)
    pair_count = flat_route.shape[0]
    one_hot = (flat_route[:, None] == jnp.arange(experts, dtype=jnp.int32)[None, :]).astype(
        jnp.int32
    )
    slot_rank = jnp.sum(one_hot * (jnp.cumsum(one_hot, axis=0) - 1), axis=1)
    slot_of = flat_route * capacity + slot_rank
    source = (
        jnp.full((experts * capacity,), pair_count, jnp.int32)
        .at[slot_of]
        .set(jnp.arange(pair_count, dtype=jnp.int32))
    )
    return (slot_of.reshape(route_rows.shape), source)


def expert_forward(row_block, weight_set, einsum_forms):
    gate_w, up_w, down_w = weight_set
    pre_gate = contract(einsum_forms[0], row_block, gate_w)
    pre_up = contract(einsum_forms[0], row_block, up_w)
    hidden = (jax.nn.silu(pre_gate) * pre_up).astype(jnp.bfloat16)
    partial_value = contract(einsum_forms[1], hidden, down_w).astype(jnp.bfloat16)
    return (partial_value, pre_gate, pre_up)


def expert_backward(grad_rows, pre_gate, pre_up, weight_set, einsum_forms):
    gate_w, up_w, down_w = weight_set
    inner_grad = contract(einsum_forms[2], grad_rows, down_w)
    sigmoid_g = jax.nn.sigmoid(pre_gate)
    activated = pre_gate * sigmoid_g
    grad_gate = (inner_grad * pre_up * sigmoid_g * (1.0 + pre_gate * (1.0 - sigmoid_g))).astype(
        jnp.bfloat16
    )
    grad_up = (inner_grad * activated).astype(jnp.bfloat16)
    return (
        contract(einsum_forms[3], grad_gate, gate_w) + contract(einsum_forms[3], grad_up, up_w)
    ).astype(jnp.bfloat16)


def body(
    tokens,
    attn_gain,
    moe_gain,
    w_qkv,
    w_out,
    w_router,
    w_gate,
    w_up,
    w_down,
    qkv_down,
    qkv_up,
    out_down,
    out_up,
    lengths,
    adapter_index,
    loss_mask,
    routes,
    upstream,
):
    n_exp = lax.axis_size("exp")
    groups = KV_HEADS // lax.axis_size("tp")
    per_group = HEADS // KV_HEADS
    experts = EXP_DEV * n_exp
    capacity = 2 * TOK_DEV * TOP // experts
    block_rows = min(512, TOK_DEV)
    blocks = TOK_DEV // block_rows
    score_scale = 1.0 / math.sqrt(HD)
    places = jnp.arange(TOK_DEV, dtype=jnp.int32)
    occupied, position, doc_ident, rank_mask = layout(lengths[0], adapter_index[0])
    mask_low = rank_mask.astype(jnp.bfloat16)
    cosine, sine_table = angles(position)
    inputs = tokens.astype(jnp.float32)
    attn_in = rms_norm(inputs, attn_gain).astype(jnp.bfloat16)
    low_q = (product(attn_in, qkv_down) * rank_mask).astype(jnp.bfloat16)
    projected = (product(attn_in, w_qkv) + product(low_q, qkv_up)).reshape(
        TOK_DEV, groups, per_group + 2, HD
    )
    query_rows = rotate(
        projected[:, :, :per_group], cosine[:, None, None], sine_table[:, None, None]
    ).astype(jnp.bfloat16)
    key_rows = rotate(projected[:, :, per_group], cosine[:, None], sine_table[:, None]).astype(
        jnp.bfloat16
    )
    val_rows = projected[:, :, per_group + 1].astype(jnp.bfloat16)

    def masked_scores(q_blk, q_place, q_ident):
        scores = contract("qgrd,kgd->grqk", q_blk, key_rows) * score_scale
        allowed = (q_ident[:, None] == doc_ident[None, :]) & (places[None, :] <= q_place[:, None])
        return jnp.where(allowed, scores, -1e30)

    def attend(pieces):
        q_blk, q_place, q_ident = pieces
        scores = masked_scores(q_blk, q_place, q_ident)
        row_max = jnp.max(scores, axis=-1, keepdims=True)
        lifted = jnp.exp(scores - row_max)
        row_total = jnp.sum(lifted, axis=-1, keepdims=True)
        weights = (lifted / row_total).astype(jnp.bfloat16)
        return (
            contract("grqk,kgd->qgrd", weights, val_rows),
            row_max[..., 0] + jnp.log(row_total[..., 0]),
        )

    query_blocks = query_rows.reshape(blocks, block_rows, groups, per_group, HD)
    place_blocks = places.reshape(blocks, block_rows)
    ident_blocks = doc_ident.reshape(blocks, block_rows)
    attended, log_totals = lax.map(attend, (query_blocks, place_blocks, ident_blocks))
    head_rows = attended.reshape(TOK_DEV, groups * per_group * HD).astype(jnp.bfloat16)
    attn_base, low_rank = (
        lax.psum(product(head_rows, w_out).astype(jnp.bfloat16), "tp").astype(jnp.float32),
        lax.psum((product(head_rows, out_down) * rank_mask).astype(jnp.bfloat16), "tp").astype(
            jnp.float32
        ),
    )
    low_o = low_rank.astype(jnp.bfloat16)
    residual = inputs + attn_base + product(low_o, out_up)
    normed = rms_norm(residual, moe_gain).astype(jnp.bfloat16)
    logits = product(normed, w_router)
    one_hot = routes[:, :, None] == jnp.arange(experts, dtype=jnp.int32)[None, None, :]
    gate_probs = jax.nn.softmax(
        jnp.sum(jnp.where(one_hot, logits[:, None, :], 0.0), axis=-1), axis=-1
    )
    slot_of, source = tables(routes, experts, capacity)
    row_of = source // TOP
    padded = jnp.concatenate([normed, jnp.zeros((1, D), jnp.bfloat16)], axis=0)
    sendbuf = padded[row_of].reshape(n_exp, EXP_DEV, capacity, D)
    weight_set = (w_gate, w_up, w_down)
    live_mask = jnp.where(occupied & (loss_mask > 0), 1.0, 0.0).astype(jnp.float32)
    cotangent = upstream.astype(jnp.float32) * live_mask[:, None]
    cot_low = cotangent.astype(jnp.bfloat16)
    outputs, pre_gate, pre_up = expert_forward(
        lax.all_to_all(sendbuf, "exp", split_axis=0, concat_axis=0, tiled=True),
        weight_set,
        LOCAL_FORMS,
    )
    returned = lax.all_to_all(outputs, "exp", split_axis=0, concat_axis=0, tiled=True)
    returned = returned.reshape(experts * capacity, D)
    moe_part = jnp.zeros((TOK_DEV, D), jnp.float32)
    gate_terms = []
    for route_slot in range(TOP):
        picked = returned[slot_of[:, route_slot]]
        moe_part = moe_part + gate_probs[:, route_slot, None] * picked.astype(jnp.float32)
        gate_terms.append(contract("td,td->t", picked, cot_low))
    moe_out, gate_grad = (
        lax.psum(moe_part.astype(jnp.bfloat16), "tp").astype(jnp.float32),
        lax.psum(jnp.stack(gate_terms, axis=1).astype(jnp.bfloat16), "tp").astype(jnp.float32),
    )
    output = (residual + moe_out).astype(jnp.bfloat16)
    slot_gate = jnp.concatenate([gate_probs.reshape(-1), jnp.zeros((1,), jnp.float32)])[source]
    cot_pad = jnp.concatenate([cot_low, jnp.zeros((1, D), jnp.bfloat16)], axis=0)
    grad_send = (
        (slot_gate[:, None] * cot_pad[row_of].astype(jnp.float32))
        .astype(jnp.bfloat16)
        .reshape(n_exp, EXP_DEV, capacity, D)
    )
    arrived_grad = lax.all_to_all(grad_send, "exp", split_axis=0, concat_axis=0, tiled=True)
    grad_back = lax.all_to_all(
        expert_backward(arrived_grad, pre_gate, pre_up, weight_set, LOCAL_FORMS),
        "exp",
        split_axis=0,
        concat_axis=0,
        tiled=True,
    )
    grad_back = grad_back.reshape(experts * capacity, D)
    normed_part = jnp.zeros((TOK_DEV, D), jnp.float32)
    for route_slot in range(TOP):
        normed_part = normed_part + grad_back[slot_of[:, route_slot]].astype(jnp.float32)
    expert_grad = lax.psum(normed_part.astype(jnp.bfloat16), "tp").astype(jnp.float32)
    chosen_grad = gate_probs * (gate_grad - jnp.sum(gate_probs * gate_grad, axis=-1, keepdims=True))
    logit_grad = jnp.sum(jnp.where(one_hot, chosen_grad[:, :, None], 0.0), axis=1).astype(
        jnp.bfloat16
    )
    normed_grad = expert_grad + product(logit_grad, w_router.T)
    residual_grad = cotangent + rms_norm_back(residual, moe_gain, normed_grad)
    branch_grad = residual_grad.astype(jnp.bfloat16)
    low_o_grad = product(branch_grad, out_up.T).astype(jnp.bfloat16) * mask_low
    out_up_part = contract("tr,td->rd", low_o, branch_grad)
    head_grad = (product(branch_grad, w_out.T) + product(low_o_grad, out_down.T)).astype(
        jnp.bfloat16
    )
    out_down_part = contract("tc,tr->cr", head_rows, low_o_grad)
    grad_blocks = head_grad.reshape(blocks, block_rows, groups, per_group, HD)

    def attend_back(carried, pieces):
        key_acc, val_acc = carried
        q_blk, q_place, q_ident, lse_blk, g_blk = pieces
        weights = jnp.exp(masked_scores(q_blk, q_place, q_ident) - lse_blk[..., None])
        weight_grad = contract("qgrd,kgd->grqk", g_blk, val_rows)
        score_grad = (
            weights * (weight_grad - jnp.sum(weights * weight_grad, axis=-1, keepdims=True))
        ).astype(jnp.bfloat16)
        query_grad = contract("grqk,kgd->qgrd", score_grad, key_rows) * score_scale
        key_acc = key_acc + contract("grqk,qgrd->kgd", score_grad, q_blk) * score_scale
        val_acc = val_acc + contract("grqk,qgrd->kgd", weights.astype(jnp.bfloat16), g_blk)
        return ((key_acc, val_acc), query_grad)

    zero_acc = jnp.zeros((TOK_DEV, groups, HD), jnp.float32)
    (key_grad, val_grad), query_grad = lax.scan(
        attend_back,
        (zero_acc, zero_acc),
        (query_blocks, place_blocks, ident_blocks, log_totals, grad_blocks),
    )
    query_grad = rotate(
        query_grad.reshape(TOK_DEV, groups, per_group, HD),
        cosine[:, None, None],
        -sine_table[:, None, None],
    )
    key_grad = rotate(key_grad, cosine[:, None], -sine_table[:, None])
    projected_grad = (
        jnp.concatenate([query_grad, key_grad[:, :, None], val_grad[:, :, None]], axis=2)
        .reshape(TOK_DEV, -1)
        .astype(jnp.bfloat16)
    )
    qkv_up_part = contract("tr,tc->rc", low_q, projected_grad)
    attn_grad, low_q_grad = (
        lax.psum(contract("tc,dc->td", projected_grad, w_qkv).astype(jnp.bfloat16), "tp").astype(
            jnp.float32
        ),
        lax.psum(contract("tc,rc->tr", projected_grad, qkv_up).astype(jnp.bfloat16), "tp").astype(
            jnp.float32
        ),
    )
    low_q_grad = low_q_grad.astype(jnp.bfloat16) * mask_low
    attn_grad = attn_grad + contract("tr,dr->td", low_q_grad, qkv_down)
    qkv_down_part = contract("td,tr->dr", attn_in, low_q_grad)
    input_grad = (residual_grad + rms_norm_back(inputs, attn_gain, attn_grad)).astype(jnp.bfloat16)
    summed = (
        lax.psum(qkv_down_part.astype(jnp.bfloat16), "exp").astype(jnp.float32),
        lax.psum(qkv_up_part.astype(jnp.bfloat16), "exp").astype(jnp.float32),
        lax.psum(out_down_part.astype(jnp.bfloat16), "exp").astype(jnp.float32),
        lax.psum(out_up_part.astype(jnp.bfloat16), "exp").astype(jnp.float32),
    )
    return (output, input_grad, summed[0], summed[1], summed[2], summed[3])


def solution(mesh):
    placed = (
        P("exp", None),
        P(),
        P(),
        P(None, "tp"),
        P("tp", None),
        P(),
        P("exp", None, "tp"),
        P("exp", None, "tp"),
        P("exp", "tp", None),
        P(),
        P(None, "tp"),
        P("tp", None),
        P(),
        P("exp", None),
        P("exp", None),
        P("exp"),
        P("exp", None),
        P("exp", None),
    )
    return jax.shard_map(
        body,
        mesh=mesh,
        in_specs=placed,
        out_specs=(P("exp", None), P("exp", None), P(), P(None, "tp"), P("tp", None), P()),
        check_vma=False,
    )
```

profile of v0, /device:TPU:0, one launch (start us, length us, event | category | flops | bytes accessed | tf_op | source)
XLA Modules:
  0.0 2122.4 jit_solution(12734274265149261734)
XLA Ops:
  13.9 3.0 fusion.127
  19.7 2.8 copy.101
  25.7 2.2 fusion.132
  30.8 2.3 fusion.60
  34.1 2.1 convolution_convert_fusion.2
  40.6 9.6 reduce-window.11
  59.5 16.4 scatter_custom_fusion
  77.4 35.5 %all-reduce.16.cloned.1.call-done = (bf16[512,128]{1,0:T(8,128)(2,1)}, bf16[512,1536]{1,0:T(8,128)(2,1)}) async-done(((bf16[512,128]{1,0:T(8,128)(2,1)}, bf16[512,1536]{1,0:T(8,128)(2,1)}), (bf16[512,128]{1,0:T(8,128)(2,1)}, bf16[512,1536]{1,0:T(8,128)(2,1)})) %all-reduce.16.cloned.1.call-update) | async-done | bytes 1703952 | tf_op jit(solution)/shard_map/psum | solution.py:192
  112.9 2.4 multiply_reduce_fusion.1
  118.7 51.0 %gather_fusion = bf16[8192,1536]{1,0:T(8,128)(2,1)} fusion(bf16[513,1536]{1,0:T(8,128)(2,1)} %concatenate.31, s32[8192]{0:T(1024)S(1)} %copy-done.40), kind=kCustom, calls=%fused_computation | custom fusion | bytes 50364416 | tf_op jit(solution)/shard_map/gather | solution.py:207
  169.7 283.3 %all_to_all.20 = bf16[8,2,512,1536]{3,2,1,0:T(8,128)(2,1)} all-to-all(bf16[8,2,512,1536]{3,2,1,0:T(8,128)(2,1)} %bitcast.204), channel_id=1, replica_groups=mesh['exp'=8,'tp'=4] {'exp'}, dimensions={0} | all-to-all | bytes 50331648 | tf_op jit(solution)/shard_map/all_to_all | solution.py:213
  453.0 13.0 fusion.5
  466.0 13.0 fusion.3
  479.0 14.9 fusion.7
  494.0 20.8 copy.111
  514.7 7.0 all-to-all-start.1
  528.5 267.1 %all-to-all-done.1 = bf16[8,2,512,1536]{3,2,1,0:T(8,128)(2,1)} async-done(((bf16[8,2,512,1536]{3,2,1,0:T(8,128)(2,1)}), bf16[8,2,512,1536]{3,2,1,0:T(8,128)(2,1)}, u32[]{:S(2)}, u32[]{:S(2)}) %all-to-all-start.1) | async-done | bytes 25165856 | tf_op jit(solution)/shard_map/all_to_all | solution.py:217
  795.6 15.1 gather_fusion.8
  810.7 16.7 gather_fusion.7
  827.4 15.9 gather_fusion.6
  843.3 16.1 gather_fusion.5
  859.4 16.0 gather_fusion.4
  875.4 16.3 gather_fusion.3
  891.8 15.9 gather_fusion.2
  907.7 15.9 gather_fusion.1
  923.6 7.0 fusion.50
  930.7 10.3 psum.81
  942.7 45.7 %gather_fusion.9 = f32[8192]{0:T(1024)S(1)} fusion(f32[4097]{0:T(1024)S(1)} %pad_maximum_fusion.4, s32[8192]{0:T(1024)} %get-tuple-element.116), kind=kCustom, calls=%fused_computation.9 | custom fusion | bytes 98304 | tf_op jit(solution)/shard_map/gather | solution.py:230
  988.4 2.7 concatenate.33
  991.0 51.0 %gather_fusion.10 = bf16[8192,1536]{1,0:T(8,128)(2,1)} fusion(bf16[513,1536]{1,0:T(8,128)(2,1)} %concatenate.33, s32[8192]{0:T(1024)S(1)} %copy-done.41), kind=kCustom, calls=%fused_computation.10 | custom fusion | bytes 50364416 | tf_op jit(solution)/shard_map/gather | solution.py:233
  1042.0 13.8 fusion
  1055.8 278.0 %all_to_all.21 = bf16[8,2,512,1536]{3,2,1,0:T(8,128)(2,1)} all-to-all(bf16[8,2,512,1536]{3,2,1,0:T(8,128)(2,1)S(1)} %fusion), channel_id=1, replica_groups=mesh['exp'=8,'tp'=4] {'exp'}, dimensions={0} | all-to-all | bytes 50331648 | tf_op jit(solution)/shard_map/all_to_all | solution.py:237
  1333.9 13.0 fusion.1
  1346.9 23.1 %fusion.56 = f32[2,8,512,1536]{3,2,1,0:T(8,128)} fusion(f32[2,8,512,128]{3,2,1,0:T(8,128)} %fusion.1, f32[2,8,512,128]{3,2,1,0:T(8,128)} %fusion.3, f32[2,8,512,128]{3,2,1,0:T(8,128)} %fusion.5, bf16[2,1536,128]{2,1,0:T(8,128)(2,1)S(1)} %copy-done.24), kind=kOutput, calls=%fused_computation.123 | convolution fusion | flops 3231711232 | bytes 63700992 | tf_op jit(solution)/shard_map/secf,edf->secd/dot_general | solution.py:30
  1370.0 28.0 %fusion.8 = bf16[8,2,512,1536]{3,2,0,1:T(8,128)(2,1)} fusion(f32[2,8,512,1536]{3,2,1,0:T(8,128)} %fusion.56, f32[2,8,512,128]{3,2,1,0:T(8,128)} %fusion.1, bf16[2,1536,128]{2,1,0:T(8,128)(2,1)S(1)} %copy-done.26, f32[2,8,512,128]{3,2,1,0:T(8,128)} %fusion.5), kind=kOutput, calls=%fused_computation.31 | convolution fusion | flops 3252682752 | bytes 84672512 | tf_op jit(solution)/shard_map/secf,edf->secd/dot_general | solution.py:30
  1398.0 20.8 copy.114
  1418.8 6.6 all-to-all-start.3
  1426.1 273.2 %all-to-all-done.3 = bf16[8,2,512,1536]{3,2,1,0:T(8,128)(2,1)} async-done(((bf16[8,2,512,1536]{3,2,1,0:T(8,128)(2,1)}), bf16[8,2,512,1536]{3,2,1,0:T(8,128)(2,1)}, u32[]{:S(2)}, u32[]{:S(2)}) %all-to-all-start.3) | async-done | bytes 25165856 | tf_op jit(solution)/shard_map/all_to_all | solution.py:238
  1699.2 16.0 gather_fusion.18
  1715.2 15.8 gather_fusion.17
  1731.0 16.2 gather_fusion.16
  1747.2 15.8 gather_fusion.15
  1763.0 15.9 gather_fusion.14
  1779.0 15.8 gather_fusion.13
  1794.8 16.0 gather_fusion.12
  1810.8 15.8 gather_fusion.11
  1826.6 7.5 add_convert_fusion.1
  1836.3 6.6 fusion.32
  1842.9 56.8 %all-reduce.10.cloned.1.call-done = bf16[512,1536]{1,0:T(8,128)(2,1)} async-done(((bf16[512,1536]{1,0:T(8,128)(2,1)}), bf16[512,1536]{1,0:T(8,128)(2,1)}) %all-reduce.10.cloned.1.call-update) | async-done | bytes 1572880 | tf_op jit(solution)/shard_map/psum | solution.py:249
  1899.8 3.3 multiply_reduce_fusion
  1903.2 2.4 subtract_add_fusion
  1910.0 2.2 fusion.9
  1917.2 2.6 convolution_convert_fusion.1
  1920.1 2.0 convolution_convert_fusion.8
  1922.2 2.2 convolution_convert_fusion.5
  1924.4 3.3 convolution_convert_fusion.3
  1927.6 117.3 %all-reduce.14.cloned.1.call-done = (bf16[512,1536]{1,0:T(8,128)(2,1)}, bf16[512,1536]{1,0:T(8,128)(2,1)}, bf16[512,128]{1,0:T(8,128)(2,1)}) async-done(((bf16[512,1536]{1,0:T(8,128)(2,1)}, bf16[512,1536]{1,0:T(8,128)(2,1)}, bf16[512,128]{1,0:T(8,128)(2,1)}), (bf16[512,1536]{1,0:T(8,128)(2,1)}, bf16[512,1536]{1,0:T(8,128)(2,1)}, bf16[512,128]{1,0:T(8,128)(2,1)})) %all-reduce.14.cloned.1.call-update) | async-done | bytes 3276816 | tf_op jit(solution)/shard_map/psum | solution.py:226
  2045.0 2.5 convolution_convert_fusion.4
  2047.5 2.7 fusion.42
  2050.2 1.9 fusion.41
  2052.2 4.0 add_convert_fusion.2
  2056.1 52.1 %all-reduce.12.cloned.1.call-done = (bf16[1536,128]{1,0:T(8,128)(2,1)}, bf16[128,640]{1,0:T(8,128)(2,1)}, bf16[384,128]{1,0:T(8,128)(2,1)}, bf16[128,1536]{1,0:T(8,128)(2,1)}) async-done(((bf16[1536,128]{1,0:T(8,128)(2,1)}, bf16[128,640]{1,0:T(8,128)(2,1)}, bf16[384,128]{1,0:T(8,128)(2,1)}, bf16[128,1536]{1,0:T(8,128)(2,1)}), (bf16[1536,128]{1,0:T(8,128)(2,1)}, bf16[128,640]{1,0:T(8,128)(2,1)}, ...) | async-done | bytes 1048592 | tf_op jit(solution)/shard_map/psum | solution.py:309
  2111.5 1.9 convert_element_type.285
  2113.4 2.0 convert_element_type.291
  (255 shorter events, 58.8 us)
Async XLA Ops:
  7.2 6.7 copy-start
  7.2 105.7 %all-reduce.16.cloned.1.call-start = ((), (), s32[]{:S(2)}) async-start(), calls=%async_computation.7 | async-start | bytes 3407872 | tf_op jit(solution)/shard_map/psum | solution.py:192
  11.3 5.7 copy-start.74
  11.3 2.6 copy-start.77
  13.9 3.0 copy-start.6
  13.9 3.1 copy-start.15
  13.9 3.1 copy-start.37
  13.9 3.1 copy-start.71
  25.6 2.4 copy-start.27
  28.0 2.7 copy-start.1
  28.0 2.7 copy-start.53
  30.8 3.3 copy-start.13
  33.1 3.2 copy-start.50
  112.9 3.1 copy-start.58
  115.3 3.5 copy-start.2
  115.9 2.8 copy-start.59
  115.9 2.8 copy-start.40
  169.7 283.3 %copy-start.23 = (bf16[2,1536,128]{2,1,0:T(8,128)(2,1)S(1)}, bf16[2,1536,128]{2,1,0:T(8,128)(2,1)}, u32[]{:S(2)}) copy-start(bf16[2,1536,128]{2,1,0:T(8,128)(2,1)} %param.24) | copy-start | bytes 2359300
  453.0 13.0 copy-start.25
  466.0 13.0 copy-start.31
  514.7 7.0 copy-start.8
  514.7 10.5 copy-start.78
  514.7 10.5 copy-start.79
  514.7 11.1 copy-start.49
  514.7 280.8 %all-to-all-start.1 = ((bf16[8,2,512,1536]{3,2,1,0:T(8,128)(2,1)}), bf16[8,2,512,1536]{3,2,1,0:T(8,128)(2,1)}, u32[]{:S(2)}, u32[]{:S(2)}) async-start(bf16[8,2,512,1536]{3,2,1,0:T(8,128)(2,1)} %copy.111), calls=%async_computation.1 | async-start | bytes 50331648 | tf_op jit(solution)/shard_map/all_to_all | solution.py:217
  521.7 6.1 copy-start.51
  527.9 267.7 %copy-start.61 = (f32[512]{0:T(512)}, f32[512]{0:T(512)S(1)}, u32[]{:S(2)}) copy-start(f32[512]{0:T(512)S(1)} %reduce_max.20) | copy-start | bytes 6148
  810.7 112.9 %copy-start.10 = (bf16[512,1536]{1,0:T(8,128)(2,1)}, bf16[512,1536]{1,0:T(8,128)(2,1)S(1)}, u32[]{:S(2)}) copy-start(bf16[512,1536]{1,0:T(8,128)(2,1)S(1)} %gather_fusion.8) | copy-start | bytes 4718596
  942.4 46.0 %copy-start.46 = (f32[512,8]{0,1:T(8,128)}, f32[512,8]{0,1:T(8,128)S(1)}, u32[]{:S(2)}) copy-start(f32[512,8]{0,1:T(8,128)S(1)} %get-tuple-element.104) | copy-start | bytes 49156
  988.3 2.7 copy-start.41
  1055.8 278.0 %copy-start.32 = (bf16[2,128,1536]{2,1,0:T(8,128)(2,1)S(1)}, bf16[2,128,1536]{2,1,0:T(8,128)(2,1)}, u32[]{:S(2)}) copy-start(bf16[2,128,1536]{2,1,0:T(8,128)(2,1)} %param.26) | copy-start | bytes 2359300
  1333.9 13.0 copy-start.24
  1346.9 23.1 %copy-start.26 = (bf16[2,1536,128]{2,1,0:T(8,128)(2,1)S(1)}, bf16[2,1536,128]{2,1,0:T(8,128)(2,1)}, u32[]{:S(2)}) copy-start(bf16[2,1536,128]{2,1,0:T(8,128)(2,1)} %param.25) | copy-start | bytes 2359300
  1418.8 6.6 copy-start.54
  1418.8 6.6 copy-start.56
  1418.8 280.4 %copy-start.64 = (s32[1024]{0:T(1024)S(1)}, s32[1024]{0:T(1024)}, u32[]{:S(2)}) copy-start(s32[1024]{0:T(1024)} %get-tuple-element.143) | copy-start | bytes 12292
  1418.8 280.4 %all-to-all-start.3 = ((bf16[8,2,512,1536]{3,2,1,0:T(8,128)(2,1)}), bf16[8,2,512,1536]{3,2,1,0:T(8,128)(2,1)}, u32[]{:S(2)}, u32[]{:S(2)}) async-start(bf16[8,2,512,1536]{3,2,1,0:T(8,128)(2,1)} %copy.114), calls=%async_computation.3 | async-start | bytes 50331648 | tf_op jit(solution)/shard_map/all_to_all | solution.py:238
  1425.4 474.4 %all-reduce.10.cloned.1.call-start = ((), (), s32[]{:S(2)}) async-start(), calls=%async_computation.4 | async-start | bytes 3145728 | tf_op jit(solution)/shard_map/psum | solution.py:249
  1699.2 16.0 copy-start.63
  1715.2 15.8 copy-start.66
  1731.0 16.2 copy-start.65
  1747.2 15.8 copy-start.68
  1763.0 16.0 copy-start.67
  1779.0 15.8 copy-start.70
  1794.8 16.0 copy-start.69
  1826.6 7.6 copy-start.47
  1826.6 9.7 copy-start.11
  1834.1 210.8 %all-reduce.14.cloned.1.call-start = ((), (), s32[]{:S(2)}) async-start(), calls=%async_computation.6 | async-start | bytes 6553600 | tf_op jit(solution)/shard_map/psum | solution.py:226
  1836.3 63.5 %copy-start.57 = (bf16[512,16]{0,1:T(8,128)(2,1)S(1)}, bf16[512,16]{0,1:T(8,128)(2,1)}, u32[]{:S(2)}) copy-start(bf16[512,16]{0,1:T(8,128)(2,1)} %select_reduce_fusion) | copy-start | bytes 49156
  1842.9 60.2 %copy-start.60 = (f32[512]{0:T(512)S(1)}, f32[512]{0:T(512)}, u32[]{:S(2)}) copy-start(f32[512]{0:T(512)} %copy-done.59) | copy-start | bytes 6148
  1842.9 60.2 %copy-start.62 = (f32[512]{0:T(512)S(1)}, f32[512]{0:T(512)}, u32[]{:S(2)}) copy-start(f32[512]{0:T(512)} %and_select_fusion) | copy-start | bytes 6148
  1842.9 60.2 %copy-start.76 = (f32[512]{0:T(512)S(1)}, f32[512]{0:T(512)}, u32[]{:S(2)}) copy-start(f32[512]{0:T(512)} %get-tuple-element.131) | copy-start | bytes 6148
  1899.8 3.4 copy-start.3
  1899.8 9.1 slice-start
  1903.2 2.5 copy-start.17
  1903.2 2.5 copy-start.21
  1903.2 5.7 slice-start.1
  1905.7 3.1 copy-start.4
  1919.8 125.2 %copy-start.7 = (bf16[512,1536]{1,0:T(8,128)(2,1)S(1)}, bf16[512,1536]{1,0:T(8,128)(2,1)}, u32[]{:S(2)}) copy-start(bf16[512,1536]{1,0:T(8,128)(2,1)} %param.18) | copy-start | bytes 4718596
  1919.8 125.2 %copy-start.72 = (f32[1536]{0:T(1024)S(1)}, f32[1536]{0:T(1024)}, u32[]{:S(2)}) copy-start(f32[1536]{0:T(1024)} %param.19) | copy-start | bytes 18436
  1919.8 125.2 %copy-start.75 = (f32[512]{0:T(512)S(1)}, f32[512]{0:T(512)}, u32[]{:S(2)}) copy-start(f32[512]{0:T(512)} %copy-done.74) | copy-start | bytes 6148
  1919.8 188.5 %all-reduce.12.cloned.1.call-start = ((), (), s32[]{:S(2)}) async-start(), calls=%async_computation.5 | async-start | bytes 2097152 | tf_op jit(solution)/shard_map/psum | solution.py:309
  2047.5 2.7 copy-start.5
  2047.5 2.7 copy-start.73
  (24 other events, 39.7 us)
Sparse Core Ops, SparseCore 0:
  36.4 76.4 all-reduce.15
  1834.3 65.4 all-reduce.9
  1919.9 125.0 all-reduce.13
  2052.3 55.9 all-reduce.11
where the time goes:
time: 2130 us; the launch traced here: 2120 us
  waiting for transfers between devices  802 us (38%)
  blocking collectives  572 us (27%)
  local copies, waits for them, and re-layouts  483 us (23%)
  matrix products  148 us (7%)
  other arithmetic  88.2 us (4%)
    all_to_all x1, blocking collectives, body(): lax.all_to_all(sendbuf, 'exp', split_axis=0, concat_axis=0, tiled=True)  283 us
    all_to_all x1, blocking collectives, body(): lax.all_to_all(grad_send, 'exp', split_axis=0, concat_axis=0, tiled=True)  278 us
    all_to_all x1, waiting for transfers between devices, body(): lax.all_to_all(expert_backward(arrived_grad, pre_gate, pre_up, weight_set...  273 us
    all_to_all x1, waiting for transfers between devices, body(): lax.all_to_all(outputs, 'exp', split_axis=0, concat_axis=0, tiled=True)  267 us
    dot_general x19, matrix products, contract(): jnp.einsum(einsum_form, left_m, right_m, preferred_element_type=jnp.float32)  131 us
    gather x8, local copies, waits for them, and re-layouts, body(): picked = returned[slot_of[:, route_slot]]  128 us
    gather x8, local copies, waits for them, and re-layouts, body(): grad_back[slot_of[:, route_slot]].astype(jnp.float32)  127 us
    psum x1, waiting for transfers between devices, body(): lax.psum(moe_part.astype(jnp.bfloat16), 'tp').astype(jnp.float32)  117 us
  transfers between devices with their start and end apart: 6, of which 6 were waited for; matrix products, arithmetic and copies ran while one was open for 3% of the time, Pallas kernels for 0%

commit v1 on v0

--- a/solution.py
+++ b/solution.py
@@ -19,7 +19,6 @@
 
 EPS = 1e-06
 ROPE_BASE = 10000.0
-LOCAL_FORMS = ("secd,edf->secf", "secf,efd->secd", "secd,efd->secf", "secf,edf->secd")
 
 
 def product(left_m, right_m):
@@ -80,43 +79,23 @@
     )
 
 
-def tables(route_rows, experts, capacity):
-    flat_route = route_rows.reshape(-1)
-    pair_count = flat_route.shape[0]
-    one_hot = (flat_route[:, None] == jnp.arange(experts, dtype=jnp.int32)[None, :]).astype(
-        jnp.int32
-    )
-    slot_rank = jnp.sum(one_hot * (jnp.cumsum(one_hot, axis=0) - 1), axis=1)
-    slot_of = flat_route * capacity + slot_rank
-    source = (
-        jnp.full((experts * capacity,), pair_count, jnp.int32)
-        .at[slot_of]
-        .set(jnp.arange(pair_count, dtype=jnp.int32))
-    )
-    return (slot_of.reshape(route_rows.shape), source)
-
-
-def expert_forward(row_block, weight_set, einsum_forms):
-    gate_w, up_w, down_w = weight_set
-    pre_gate = contract(einsum_forms[0], row_block, gate_w)
-    pre_up = contract(einsum_forms[0], row_block, up_w)
-    hidden = (jax.nn.silu(pre_gate) * pre_up).astype(jnp.bfloat16)
-    partial_value = contract(einsum_forms[1], hidden, down_w).astype(jnp.bfloat16)
-    return (partial_value, pre_gate, pre_up)
-
-
-def expert_backward(grad_rows, pre_gate, pre_up, weight_set, einsum_forms):
-    gate_w, up_w, down_w = weight_set
-    inner_grad = contract(einsum_forms[2], grad_rows, down_w)
+def moe(normed, cot_low, gates, gate_up, down):
+    width = down.shape[1]
+    both = contract("td,edf->tef", normed, gate_up)
+    pre_gate = both[:, :, :width]
+    pre_up = both[:, :, width:]
     sigmoid_g = jax.nn.sigmoid(pre_gate)
     activated = pre_gate * sigmoid_g
-    grad_gate = (inner_grad * pre_up * sigmoid_g * (1.0 + pre_gate * (1.0 - sigmoid_g))).astype(
-        jnp.bfloat16
-    )
-    grad_up = (inner_grad * activated).astype(jnp.bfloat16)
-    return (
-        contract(einsum_forms[3], grad_gate, gate_w) + contract(einsum_forms[3], grad_up, up_w)
-    ).astype(jnp.bfloat16)
+    hidden = (activated * pre_up).astype(jnp.bfloat16).astype(jnp.float32)
+    inner_raw = contract("td,efd->tef", cot_low, down)
+    gate_part = jnp.sum(hidden * inner_raw, axis=-1)
+    moe_part = contract("tef,efd->td", (gates[:, :, None] * hidden).astype(jnp.bfloat16), down)
+    inner_grad = inner_raw * gates[:, :, None]
+    grad_gate = inner_grad * pre_up * sigmoid_g * (1.0 + pre_gate * (1.0 - sigmoid_g))
+    grad_up = inner_grad * activated
+    grad_both = jnp.concatenate([grad_gate, grad_up], axis=2).astype(jnp.bfloat16)
+    normed_part = contract("tef,edf->td", grad_both, gate_up)
+    return (moe_part, gate_part, normed_part)
 
 
 def body(
@@ -143,7 +122,8 @@
     groups = KV_HEADS // lax.axis_size("tp")
     per_group = HEADS // KV_HEADS
     experts = EXP_DEV * n_exp
-    capacity = 2 * TOK_DEV * TOP // experts
+    gate_up = lax.all_gather(jnp.concatenate([w_gate, w_up], axis=2), "exp", axis=0, tiled=True)
+    down = lax.all_gather(w_down, "exp", axis=0, tiled=True)
     block_rows = min(512, TOK_DEV)
     blocks = TOK_DEV // block_rows
     score_scale = 1.0 / math.sqrt(HD)
@@ -198,60 +178,21 @@
     normed = rms_norm(residual, moe_gain).astype(jnp.bfloat16)
     logits = product(normed, w_router)
     one_hot = routes[:, :, None] == jnp.arange(experts, dtype=jnp.int32)[None, None, :]
-    gate_probs = jax.nn.softmax(
-        jnp.sum(jnp.where(one_hot, logits[:, None, :], 0.0), axis=-1), axis=-1
-    )
-    slot_of, source = tables(routes, experts, capacity)
-    row_of = source // TOP
-    padded = jnp.concatenate([normed, jnp.zeros((1, D), jnp.bfloat16)], axis=0)
-    sendbuf = padded[row_of].reshape(n_exp, EXP_DEV, capacity, D)
-    weight_set = (w_gate, w_up, w_down)
+    routed = jnp.any(one_hot, axis=1)
+    gates = jax.nn.softmax(jnp.where(routed, logits, -1e30), axis=-1)
     live_mask = jnp.where(occupied & (loss_mask > 0), 1.0, 0.0).astype(jnp.float32)
     cotangent = upstream.astype(jnp.float32) * live_mask[:, None]
     cot_low = cotangent.astype(jnp.bfloat16)
-    outputs, pre_gate, pre_up = expert_forward(
-        lax.all_to_all(sendbuf, "exp", split_axis=0, concat_axis=0, tiled=True),
-        weight_set,
-        LOCAL_FORMS,
-    )
-    returned = lax.all_to_all(outputs, "exp", split_axis=0, concat_axis=0, tiled=True)
-    returned = returned.reshape(experts * capacity, D)
-    moe_part = jnp.zeros((TOK_DEV, D), jnp.float32)
-    gate_terms = []
-    for route_slot in range(TOP):
-        picked = returned[slot_of[:, route_slot]]
-        moe_part = moe_part + gate_probs[:, route_slot, None] * picked.astype(jnp.float32)
-        gate_terms.append(contract("td,td->t", picked, cot_low))
-    moe_out, gate_grad = (
-        lax.psum(moe_part.astype(jnp.bfloat16), "tp").astype(jnp.float32),
-        lax.psum(jnp.stack(gate_terms, axis=1).astype(jnp.bfloat16), "tp").astype(jnp.float32),
-    )
+    moe_part, gate_part, normed_part = moe(normed, cot_low, gates, gate_up, down)
+    logit_grad = (
+        gates * (gate_part - jnp.sum(gates * gate_part, axis=-1, keepdims=True))
+    ).astype(jnp.bfloat16)
+    normed_part = (normed_part + product(logit_grad, w_router.T)).astype(jnp.bfloat16)
+    normed_sum = lax.psum(normed_part, "tp")
+    normed_sum, moe_part = lax.optimization_barrier((normed_sum, moe_part.astype(jnp.bfloat16)))
+    normed_grad = normed_sum.astype(jnp.float32)
+    moe_out = lax.psum(moe_part, "tp").astype(jnp.float32)
     output = (residual + moe_out).astype(jnp.bfloat16)
-    slot_gate = jnp.concatenate([gate_probs.reshape(-1), jnp.zeros((1,), jnp.float32)])[source]
-    cot_pad = jnp.concatenate([cot_low, jnp.zeros((1, D), jnp.bfloat16)], axis=0)
-    grad_send = (
-        (slot_gate[:, None] * cot_pad[row_of].astype(jnp.float32))
-        .astype(jnp.bfloat16)
-        .reshape(n_exp, EXP_DEV, capacity, D)
-    )
-    arrived_grad = lax.all_to_all(grad_send, "exp", split_axis=0, concat_axis=0, tiled=True)
-    grad_back = lax.all_to_all(
-        expert_backward(arrived_grad, pre_gate, pre_up, weight_set, LOCAL_FORMS),
-        "exp",
-        split_axis=0,
-        concat_axis=0,
-        tiled=True,
-    )
-    grad_back = grad_back.reshape(experts * capacity, D)
-    normed_part = jnp.zeros((TOK_DEV, D), jnp.float32)
-    for route_slot in range(TOP):
-        normed_part = normed_part + grad_back[slot_of[:, route_slot]].astype(jnp.float32)
-    expert_grad = lax.psum(normed_part.astype(jnp.bfloat16), "tp").astype(jnp.float32)
-    chosen_grad = gate_probs * (gate_grad - jnp.sum(gate_probs * gate_grad, axis=-1, keepdims=True))
-    logit_grad = jnp.sum(jnp.where(one_hot, chosen_grad[:, :, None], 0.0), axis=1).astype(
-        jnp.bfloat16
-    )
-    normed_grad = expert_grad + product(logit_grad, w_router.T)
     residual_grad = cotangent + rms_norm_back(residual, moe_gain, normed_grad)
     branch_grad = residual_grad.astype(jnp.bfloat16)
     low_o_grad = product(branch_grad, out_up.T).astype(jnp.bfloat16) * mask_low

time: 2130 us -> 488 us (0.23)
  blocking collectives: 572 us -> 0 us
  waiting for transfers between devices: 802 us -> 329 us
  local copies, waits for them, and re-layouts: 483 us -> 11.6 us
  matrix products: 148 us -> 84.2 us
  other arithmetic: 88.2 us -> 38.4 us
    all_to_all x2 -> x0, blocking collectives: 561 us -> none  [the longest x1 283 us: body(): lax.all_to_all(sendbuf, 'exp', split_axis=0, concat_axis=0, tiled=True)]
    all_to_all x2 -> x0, waiting for transfers between devices: 540 us -> none  [the longest x1 273 us: body(): lax.all_to_all(expert_backward(arrived_grad, pre_gate, pre_up, weight_set...]
    gather x19 -> x0, local copies, waits for them, and re-layouts: 403 us -> none  [the longest x8 128 us: body(): picked = returned[slot_of[:, route_slot]]]
    dot_general x19 -> x17, matrix products: 131 us -> 69.6 us  [contract(): jnp.einsum(einsum_form, left_m, right_m, preferred_element_type=jnp.float32)]
    convert_element_type x2 -> x0, local copies, waits for them, and re-layouts: 41.5 us -> none  [the longest x1 20.8 us: expert_forward(): contract(einsum_forms[1], hidden, down_w).astype(jnp.bfloat16)]
    psum x1, waiting for transfers between devices: 35.5 us -> 71.8 us  [body(): lax.psum((product(head_rows, out_down) * rank_mask).astype(jnp.bfloat16),...]
    convert_element_type x6 -> x0, other arithmetic: 32.9 us -> none  [the longest x1 13.8 us: body(): grad_send = (slot_gate[:, None] * cot_pad[row_of].astype(jnp.float32)).as...]
    all_gather x0 -> x2, waiting for transfers between devices: none -> 29.8 us  [the longest x1 29.8 us: body(): down = lax.all_gather(w_down, 'exp', axis=0, tiled=True)]
  transfers between devices with their start and end apart: 6 -> 6, of which waited for: 6 -> 5; matrix products, arithmetic and copies ran while one was open for 3% -> 9% of each run, Pallas kernels for 0% -> 0%
where the time goes in v1:
time: 488 us; the launch traced here: 480 us
  waiting for transfers between devices  329 us (67%)
  matrix products  84.2 us (17%)
  other arithmetic  38.4 us (8%)
  between operations  16.6 us (3%)
  local copies, waits for them, and re-layouts  11.6 us (2%)
    psum x1, waiting for transfers between devices, body(): moe_out = lax.psum(moe_part, 'tp').astype(jnp.float32)  118 us
    psum x1, waiting for transfers between devices, body(): lax.psum((product(head_rows, out_down) * rank_mask).astype(jnp.bfloat16),...  71.8 us
    dot_general x17, matrix products, contract(): jnp.einsum(einsum_form, left_m, right_m, preferred_element_type=jnp.float32)  69.6 us
    psum x1, waiting for transfers between devices, body(): normed_sum = lax.psum(normed_part, 'tp')  60.2 us
    psum x1, waiting for transfers between devices, body(): lax.psum(qkv_down_part.astype(jnp.bfloat16), 'exp').astype(jnp.float32)  49.2 us
    all_gather x1, waiting for transfers between devices, body(): down = lax.all_gather(w_down, 'exp', axis=0, tiled=True)  29.8 us
    dot_general x11, matrix products, product(): return jnp.dot(left_m, right_m, preferred_element_type=jnp.float32)  14.5 us
  transfers between devices with their start and end apart: 6, of which 5 were waited for; matrix products, arithmetic and copies ran while one was open for 9% of the time, Pallas kernels for 0%

profile of v1, /device:TPU:0, one launch (start us, length us, event | category | flops | bytes accessed | tf_op | source)
XLA Modules:
  0.0 480.4 jit_solution(3966912119440392669)
XLA Ops:
  8.1 1.0 reduce-window.4
  9.0 0.7 fusion.69
  9.8 0.8 select_reduce_fusion
  10.6 0.8 copy.68
  11.4 1.8 fusion.18
  13.2 0.6 multiply_multiply_fusion
  13.8 3.0 fusion.80
  16.9 0.6 fusion.51
  17.5 0.6 copy-done.28
  18.2 1.4 convolution_add_fusion.3
  19.6 2.8 copy.69
  22.4 1.0 copy_bitcast_fusion
  23.4 0.9 fusion.64
  24.3 1.3 subtract_convert_fusion.1
  25.9 1.2 fusion.83
  27.2 0.9 fusion.3
  28.1 1.8 copy-done.1
  29.9 2.2 fusion.40
  32.2 2.1 convolution_convert_fusion.1
  34.3 1.0 fusion.47
  35.4 2.7 pad_maximum_fusion
  38.1 0.5 all-gather.3.cloned.1.call-update
  38.7 0.8 fusion.57
  39.5 0.6 and_select_fusion
  40.1 71.8 %all-reduce.14.cloned.1.call-done = (bf16[512,128]{1,0:T(8,128)(2,1)}, bf16[512,1536]{1,0:T(8,128)(2,1)}) async-done(((bf16[512,128]{1,0:T(8,128)(2,1)}, bf16[512,1536]{1,0:T(8,128)(2,1)}), (bf16[512,128]{1,0:T(8,128)(2,1)}, bf16[512,1536]{1,0:T(8,128)(2,1)})) %all-reduce.14.cloned.1.call-update) | async-done | bytes 1703952 | tf_op jit(solution)/shard_map/psum | solution.py:172
  111.9 2.4 multiply_reduce_fusion.1
  114.3 0.6 multiply_multiply_fusion.1
  114.9 1.0 copy-done.2
  116.0 0.6 fusion.84
  116.6 0.6 copy-done.33
  117.3 13.0 %fusion.36 = f32[512,16,256]{0,2,1:T(8,128)} fusion(bf16[16,1536,256]{2,1,0:T(8,128)(2,1)} %all-gather.5.cloned.1.call-done, f32[512,1536]{1,0:T(8,128)} %copy-done.2, f32[1536]{0:T(1024)S(1)} %copy-done.41, f32[512]{0:T(512)} %copy-done.45), kind=kOutput, calls=%fused_computation.64 | convolution fusion | flops 6444810240 | bytes 24125440 | tf_op jit(solution)/shard_map/td,edf->tef/dot_general | solution.py:29
  130.3 29.8 %all-gather.3.cloned.1.call-done = bf16[16,128,1536]{2,1,0:T(8,128)(2,1)} async-done(((bf16[2,128,1536]{2,1,0:T(8,128)(2,1)}), bf16[16,128,1536]{2,1,0:T(8,128)(2,1)}) %all-gather.3.cloned.1.call-update) | async-done | bytes 6291472 | tf_op jit(solution)/shard_map/all_gather | solution.py:126
  160.1 11.9 %fusion.5 = (f32[512,16]{0,1:T(8,128)S(1)}, bf16[512,16,128]{0,2,1:T(8,128)(2,1)}, f32[512,16,128]{0,2,1:T(8,128)S(1)}) fusion(f32[512,16,256]{0,2,1:T(8,128)} %fusion.36, bf16[16,128,1536]{2,1,0:T(8,128)(2,1)} %all-gather.3.cloned.1.call-done, bf16[512,1536]{1,0:T(8,128)(2,1)} %param.35, f32[512]{0:T(512)S(1)} %copy-done.55), kind=kOutput, calls=%fused_computation.18 | convolution fusion | flops 3233013760 | bytes 22579200 | tf_op jit(solution)/shard_map/td,efd->tef/dot_general | solution.py:29
  172.1 2.6 multiply_convert_fusion.2
  174.7 9.4 %fusion.13 = f32[512,1536]{1,0:T(8,128)S(1)} fusion(bf16[16,1536,256]{2,1,0:T(8,128)(2,1)} %all-gather.5.cloned.1.call-done, bf16[512,16,128]{0,2,1:T(8,128)(2,1)S(1)} %get-tuple-element.96, bf16[512,16,128]{0,2,1:T(8,128)(2,1)S(1)} %get-tuple-element.95), kind=kOutput, calls=%fused_computation.33 | convolution fusion | flops 6450839552 | bytes 19922944 | tf_op jit(solution)/shard_map/tef,edf->td/dot_general | solution.py:29
  184.1 1.7 fusion.30
  186.1 0.7 log_add_fusion
  186.9 8.1 %fusion.29 = bf16[512,1536]{1,0:T(8,128)(2,1)} fusion(bf16[16,128,1536]{2,1,0:T(8,128)(2,1)} %all-gather.3.cloned.1.call-done, bf16[512,16,128]{0,2,1:T(8,128)(2,1)} %get-tuple-element.94, f32[512,16]{0,1:T(8,128)} %copy-done.32), kind=kOutput, calls=%fused_computation.54 | convolution fusion | flops 3225157632 | bytes 9994240 | tf_op jit(solution)/shard_map/tef,efd->td/dot_general | solution.py:29
  194.9 60.2 %all-reduce.8.cloned.1.call-done = bf16[512,1536]{1,0:T(8,128)(2,1)} async-done(((bf16[512,1536]{1,0:T(8,128)(2,1)}), bf16[512,1536]{1,0:T(8,128)(2,1)}) %all-reduce.8.cloned.1.call-update) | async-done | bytes 1572880 | tf_op jit(solution)/shard_map/psum | solution.py:191
  255.2 3.0 multiply_reduce_fusion
  259.0 2.6 subtract_add_fusion
  261.6 0.6 fusion.55
  262.2 0.6 copy-done.20
  263.1 0.8 copy-done.10
  263.9 0.8 fusion.41
  264.8 2.9 fusion
  267.7 2.6 fusion.2
  270.4 0.7 fusion.39
  271.4 1.1 fusion.46
  272.5 1.1 fusion.52
  273.9 2.6 convolution_convert_fusion
  276.5 1.3 convolution_convert_fusion.5
  277.9 1.9 convolution_convert_fusion.7
  279.8 2.2 convolution_convert_fusion.4
  282.0 3.5 convolution_convert_fusion.2
  285.4 117.5 %all-reduce.12.cloned.1.call-done = (bf16[512,1536]{1,0:T(8,128)(2,1)}, bf16[512,1536]{1,0:T(8,128)(2,1)}, bf16[512,128]{1,0:T(8,128)(2,1)}) async-done(((bf16[512,1536]{1,0:T(8,128)(2,1)}, bf16[512,1536]{1,0:T(8,128)(2,1)}, bf16[512,128]{1,0:T(8,128)(2,1)}), (bf16[512,1536]{1,0:T(8,128)(2,1)}, bf16[512,1536]{1,0:T(8,128)(2,1)}, bf16[512,128]{1,0:T(8,128)(2,1)})) %all-reduce.12.cloned.1.call-update) | async-done | bytes 3276816 | tf_op jit(solution)/shard_map/psum | solution.py:194
  403.0 2.5 convolution_convert_fusion.3
  405.5 4.1 fusion.25
  409.7 6.6 %fusion.24 = (bf16[512,1536]{1,0:T(8,128)(2,1)}, bf16[512,1536]{1,0:T(8,128)(2,1)}) fusion(f32[512,1536]{1,0:T(8,128)} %copy-done.4, bf16[512,1536]{1,0:T(8,128)(2,1)S(1)} %copy-done.5, f32[512,1536]{1,0:T(8,128)} %get-tuple-element.122, f32[512]{0:T(512)S(1)} %broadcast_multiply_fusion, f32[512]{0:T(512)S(1)} %copy-done.51, f32[512]{0:T(512)S(1)} %copy-done.53, ...), kind=kLoop, calls=%fused_computation.42 | loop fusion | flops 7864320 | bytes 15734784 | tf_op jit(solution)/shard_map/convert_element_type | solution.py:248
  416.3 49.2 %all-reduce.10.cloned.1.call-done = (bf16[1536,128]{1,0:T(8,128)(2,1)}, bf16[128,640]{1,0:T(8,128)(2,1)}, bf16[384,128]{1,0:T(8,128)(2,1)}, bf16[128,1536]{1,0:T(8,128)(2,1)}) async-done(((bf16[1536,128]{1,0:T(8,128)(2,1)}, bf16[128,640]{1,0:T(8,128)(2,1)}, bf16[384,128]{1,0:T(8,128)(2,1)}, bf16[128,1536]{1,0:T(8,128)(2,1)}), (bf16[1536,128]{1,0:T(8,128)(2,1)}, bf16[128,640]{1,0:T(8,128)(2,1)}, ...) | async-done | bytes 1048592 | tf_op jit(solution)/shard_map/psum | solution.py:250
  465.5 1.9 convert_element_type.181
  467.4 2.0 convert_element_type.187
  469.4 1.7 convert_element_type.183
  471.0 1.6 convert_element_type.185
  (148 shorter events, 2.9 us)
Async XLA Ops:
  8.0 5.8 %copy-start = (bf16[1536,640]{1,0:T(8,128)(2,1)S(1)}, bf16[1536,640]{1,0:T(8,128)(2,1)}, u32[]{:S(2)}) copy-start(bf16[1536,640]{1,0:T(8,128)(2,1)} %param.21) | copy-start | bytes 5898244
  8.0 103.9 %all-reduce.14.cloned.1.call-start = ((), (), s32[]{:S(2)}) async-start(), calls=%async_computation.5 | async-start | bytes 3407872 | tf_op jit(solution)/shard_map/psum | solution.py:172
  9.8 15.9 %copy-start.57 = (pred[512]{0:T(512)(128)(4,1)}, pred[512]{0:T(512)(128)(4,1)S(1)}, u32[]{:S(2)}) copy-start(pred[512]{0:T(512)(128)(4,1)S(1)} %fusion.77) | copy-start | bytes 1540
  13.8 3.0 copy-start.52
  13.8 3.0 copy-start.5
  13.8 3.1 copy-start.11
  13.8 3.1 copy-start.29
  13.8 3.1 copy-start.49
  16.9 1.3 copy-start.25
  24.3 1.6 copy-start.17
  25.6 1.5 copy-start.21
  25.6 1.5 copy-start.23
  25.6 1.5 copy-start.35
  25.6 1.5 copy-start.37
  27.2 2.7 copy-start.1
  27.2 2.7 copy-start.43
  29.9 2.2 copy-start.44
  29.9 2.3 copy-start.9
  32.1 2.2 copy-start.14
  32.1 2.2 copy-start.12
  32.1 2.2 copy-start.30
  35.3 4.2 copy-start.58
  35.3 4.2 copy-start.59
  35.3 82.0 %all-gather.5.cloned.1.call-start = ((), (), s32[]{:S(2)}) async-start(), calls=%async_computation.1 | async-start | bytes 14155776 | tf_op jit(solution)/shard_map/all_gather | solution.py:125
  38.1 122.0 %all-gather.3.cloned.1.call-start = ((), (), s32[]{:S(2)}) async-start(), calls=%async_computation | async-start | bytes 7077888 | tf_op jit(solution)/shard_map/all_gather | solution.py:126
  38.7 216.5 %all-reduce.8.cloned.1.call-start = ((), (), s32[]{:S(2)}) async-start(), calls=%async_computation.2 | async-start | bytes 3145728 | tf_op jit(solution)/shard_map/psum | solution.py:191
  111.9 4.1 copy-start.39
  111.9 4.1 copy-start.41
  114.3 1.7 copy-start.2
  114.9 1.7 copy-start.45
  117.3 42.8 %copy-start.55 = (f32[512]{0:T(512)S(1)}, f32[512]{0:T(512)}, u32[]{:S(2)}) copy-start(f32[512]{0:T(512)} %and_select_fusion) | copy-start | bytes 6148
  130.3 41.7 %copy-start.48 = (f32[512]{0:T(512)S(1)}, f32[512]{0:T(512)}, u32[]{:S(2)}) copy-start(f32[512]{0:T(512)} %copy-done.47) | copy-start | bytes 6148
  160.1 11.9 %copy-start.34 = (f32[512,16]{0,1:T(8,128)S(1)}, f32[512,16]{0,1:T(8,128)}, u32[]{:S(2)}) copy-start(f32[512,16]{0,1:T(8,128)} %copy-done.33) | copy-start | bytes 98308
  160.1 12.0 %copy-start.6 = (f32[512,16,256]{0,2,1:T(8,128)S(1)}, f32[512,16,256]{0,2,1:T(8,128)}, u32[]{:S(2)}) copy-start(f32[512,16,256]{0,2,1:T(8,128)} %fusion.36) | copy-start | bytes 25165828
  172.0 12.1 %copy-start.32 = (f32[512,16]{0,1:T(8,128)}, f32[512,16]{0,1:T(8,128)S(1)}, u32[]{:S(2)}) copy-start(f32[512,16]{0,1:T(8,128)S(1)} %get-tuple-element.92) | copy-start | bytes 98308
  174.7 9.4 %copy-start.40 = (bf16[1536,16]{0,1:T(8,128)(2,1)S(1)}, bf16[1536,16]{0,1:T(8,128)(2,1)}, u32[]{:S(2)}) copy-start(bf16[1536,16]{0,1:T(8,128)(2,1)} %param.23) | copy-start | bytes 147460
  185.9 217.1 %all-reduce.12.cloned.1.call-start = ((), (), s32[]{:S(2)}) async-start(), calls=%async_computation.4 | async-start | bytes 6553600 | tf_op jit(solution)/shard_map/psum | solution.py:194
  255.2 3.3 copy-start.3
  255.2 3.8 copy-start.7
  255.2 3.8 copy-start.42
  255.2 3.8 copy-start.46
  255.2 3.8 copy-start.54
  255.2 3.8 copy-start.56
  258.9 2.6 copy-start.13
  259.0 2.6 copy-start.19
  259.0 5.8 %slice-start = ((s8[6291456]{0:T(1024)(128)(4,1)}), s8[4194304]{0:T(1024)(128)(4,1)S(1)}, s32[]{:S(2)}) async-start(s8[6291456]{0:T(1024)(128)(4,1)} %bitcast.118), calls=%async_computation.6 | async-start | bytes 8388608
  261.6 3.1 copy-start.4
  261.6 1.3 copy-start.31
  261.6 2.3 copy-start.10
  261.6 3.2 slice-start.1
  264.7 3.0 copy-start.15
  267.7 2.6 copy-start.36
  267.7 2.6 copy-start.38
  270.4 0.9 copy-start.22
  270.4 1.0 copy-start.24
  270.4 2.1 copy-start.16
  272.5 1.1 copy-start.18
  272.5 1.1 copy-start.27
  273.9 2.6 copy-start.8
  273.9 2.6 copy-start.26
  277.8 125.2 %copy-start.50 = (f32[1536]{0:T(1024)S(1)}, f32[1536]{0:T(1024)}, u32[]{:S(2)}) copy-start(f32[1536]{0:T(1024)} %param.19) | copy-start | bytes 18436
  277.8 125.2 %copy-start.53 = (f32[512]{0:T(512)S(1)}, f32[512]{0:T(512)}, u32[]{:S(2)}) copy-start(f32[512]{0:T(512)} %copy-done.52) | copy-start | bytes 6148
  277.8 187.7 %all-reduce.10.cloned.1.call-start = ((), (), s32[]{:S(2)}) async-start(), calls=%async_computation.3 | async-start | bytes 2097152 | tf_op jit(solution)/shard_map/psum | solution.py:250
  405.5 4.2 copy-start.51
  (4 other events, 2.5 us)
Sparse Core Ops, SparseCore 0:
  35.4 76.4 all-reduce.13
  186.0 69.1 all-reduce.7
  277.9 125.0 all-reduce.11
Sparse Core Ops, SparseCore 1:
  38.3 74.6 all-gather.4
  114.7 45.3 all-gather.2
  409.8 55.7 all-reduce.9

commit v2 on v1

--- a/solution.py
+++ b/solution.py
@@ -1,8 +1,12 @@
+import functools
 import math
 
 import jax
 import jax.numpy as jnp
+import numpy as np
 from jax import lax
+from jax.experimental import pallas as pl
+from jax.experimental.pallas import tpu as pltpu
 from jax.sharding import PartitionSpec as P
 
 D = 1536
@@ -15,10 +19,631 @@
 EXP_DEV = 2
 DOCS = 4
 TOK_DEV = 512
-
-
+FF = 512
 EPS = 1e-06
 ROPE_BASE = 10000.0
+
+PER = HEADS // KV_HEADS
+LANES = 128
+ROWS = 128
+F32 = jnp.float32
+BF16 = jnp.bfloat16
+MIB = 2**20
+NT = (((1,), (1,)), ((), ()))
+TN = (((0,), (0,)), ((), ()))
+IN_VMEM = pl.BlockSpec(memory_space=pltpu.VMEM)
+IN_SMEM = pl.BlockSpec(memory_space=pltpu.SMEM)
+IN_HBM = pl.BlockSpec(memory_space=pl.ANY)
+
+
+def dot(left, right):
+    return jnp.dot(left, right, preferred_element_type=F32)
+
+
+def dot_nt(left, right):
+    return lax.dot_general(left, right, NT, preferred_element_type=F32)
+
+
+def dot_tn(left, right):
+    return lax.dot_general(left, right, TN, preferred_element_type=F32)
+
+
+def shape(dims, dtype):
+    return jax.ShapeDtypeStruct(dims, dtype)
+
+
+def turn_tables(rows):
+    half = HD // 2
+    frequency = np.exp(-math.log(ROPE_BASE) * np.arange(half, dtype=np.float64) * 2.0 / HD)
+    turned = np.arange(rows, dtype=np.float64)[:, None] * frequency[None, :]
+    cosine, sine = np.cos(turned), np.sin(turned)
+    return (
+        jnp.asarray(np.concatenate([cosine] * 4, axis=1), F32),
+        jnp.asarray(np.concatenate([-sine, sine, -sine, sine], axis=1), F32),
+    )
+
+
+def turned_pieces(groups):
+    return [piece < PER + 1 for _ in range(groups) for piece in range(PER + 2)]
+
+
+def turn(joined, cosine, sine, flags):
+    lane = lax.broadcasted_iota(jnp.int32, cosine.shape, 1)
+    front = (lane & 32) == 0
+    left = lane < HD
+    columns = []
+    for at in range(joined.shape[1] // LANES):
+        column = joined[:, at * LANES : (at + 1) * LANES]
+        swapped = jnp.where(front, pltpu.roll(column, 96, 1), pltpu.roll(column, 32, 1))
+        rotated = column * cosine + swapped * sine
+        if not (flags[2 * at] and flags[2 * at + 1]):
+            rotated = jnp.where(left if flags[2 * at] else jnp.logical_not(left), rotated, column)
+        columns.append(rotated)
+    return columns
+
+
+def first_keys(length_ref, rows):
+    row = lax.broadcasted_iota(jnp.int32, (rows, 1), 0)
+    begin = jnp.zeros((rows, 1), jnp.int32)
+    end = 0
+    for doc in range(DOCS):
+        if doc:
+            begin = jnp.where(row >= end, end, begin)
+        end = end + length_ref[0, doc]
+    return jnp.where(row >= end, row, begin)
+
+
+def adapter_mask(length_ref, index_ref, rows, width):
+    row = lax.broadcasted_iota(jnp.int32, (rows, width), 0)
+    adapter = lax.shift_right_logical(lax.broadcasted_iota(jnp.int32, (rows, width), 1), 4)
+    mask = jnp.zeros((rows, width), F32)
+    begin = 0
+    for doc in range(DOCS):
+        end = begin + length_ref[0, doc]
+        inside = (row >= begin) & (row < end) & (adapter == index_ref[0, doc])
+        mask = jnp.where(inside, 1.0, mask)
+        begin = end
+    return mask
+
+
+def seen_block(first, block):
+    keys = (block + 1) * ROWS
+    row = lax.broadcasted_iota(jnp.int32, (ROWS, keys), 0) + block * ROWS
+    key = lax.broadcasted_iota(jnp.int32, (ROWS, keys), 1)
+    seen = (key <= row) & (key >= first[block * ROWS : (block + 1) * ROWS])
+    return jnp.concatenate([seen] * PER, axis=0)
+
+
+def store_heads(columns, slot, q_s, k_s, v_s):
+    scale = 1.0 / math.sqrt(HD)
+    blocks = q_s.shape[1]
+    for at, column in enumerate(columns):
+        halves = (column[:, :HD], pltpu.roll(column, HD, 1)[:, :HD])
+        for piece, part in zip((2 * at, 2 * at + 1), halves):
+            group, kind = divmod(piece, PER + 2)
+            if kind == PER:
+                k_s[slot + group] = part.astype(BF16)
+            elif kind == PER + 1:
+                v_s[slot + group] = part.astype(BF16)
+            else:
+                part = (part * scale).astype(BF16)
+                for block in range(blocks):
+                    q_s[slot + group, block, kind * ROWS : (kind + 1) * ROWS, :] = part[
+                        block * ROWS : (block + 1) * ROWS
+                    ]
+
+
+def pack_kernel(
+    n_exp, place_ref, gate, up, down, w_qkv, qkv_up, w_out, out_down, experts, shares, sem
+):
+    width = gate.shape[2]
+    copies = []
+    for expert in range(gate.shape[0]):
+        copies.append((gate.at[expert], experts.at[expert, :, :width]))
+        copies.append((up.at[expert], experts.at[expert, :, width : 2 * width]))
+        for at in range(D // LANES):
+            lanes = slice(at * LANES, (at + 1) * LANES)
+            copies.append((down.at[expert, :, lanes], experts.at[expert, lanes, 2 * width :]))
+    qkv_rows, up_rows, out_rows = share_rows(n_exp, w_out.shape[0])
+    place = place_ref[0]
+    own_qkv = pl.ds(pl.multiple_of(place * qkv_rows, 16), qkv_rows)
+    own_up = pl.ds(pl.multiple_of(place * up_rows, 16), up_rows)
+    own_out = pl.ds(pl.multiple_of(place * out_rows, 16), out_rows)
+    wide = w_qkv.shape[1]
+    copies.append((w_qkv.at[own_qkv, :], shares.at[:qkv_rows, :]))
+    at = qkv_rows + up_rows
+    copies.append((qkv_up.at[own_up, :], shares.at[qkv_rows:at, :]))
+    for left in range(0, D, wide):
+        taken = min(wide, D - left)
+        target = shares.at[at : at + out_rows, :taken]
+        copies.append((w_out.at[own_out, left : left + taken], target))
+        at += out_rows
+    at -= out_rows
+    copies.append((out_down.at[own_out, :], shares.at[at : at + out_rows, taken : taken + LANES]))
+    started = [
+        pltpu.make_async_copy(source, target, sem.at[number])
+        for number, (source, target) in enumerate(copies)
+    ]
+    for copy in started:
+        copy.start()
+    for copy in started:
+        copy.wait()
+
+
+def share_rows(n_exp, heads_wide):
+    return (D // n_exp, LANES // n_exp, heads_wide // n_exp)
+
+
+def pack(place, w_gate, w_up, w_down, w_qkv, qkv_up, w_out, out_down, n_exp):
+    count, _, width = w_gate.shape
+    qkv_rows, up_rows, out_rows = share_rows(n_exp, w_out.shape[0])
+    wide = w_qkv.shape[1]
+    pieces = -(-D // wide)
+    copies = count * (2 + D // LANES) + 3 + pieces
+    return pl.pallas_call(
+        functools.partial(pack_kernel, n_exp),
+        in_specs=[IN_SMEM] + [IN_HBM] * 7,
+        out_specs=[IN_HBM] * 2,
+        out_shape=[
+            shape((count, D, 3 * width), BF16),
+            shape((qkv_rows + up_rows + pieces * out_rows, wide), BF16),
+        ],
+        scratch_shapes=[pltpu.SemaphoreType.DMA((copies,))],
+        name="pack_weights",
+    )(place, w_gate, w_up, w_down, w_qkv, qkv_up, w_out, out_down)
+
+
+def forward_kernel(
+    length_ref, index_ref, tokens_hbm, gain_hbm, w_qkv_hbm, qkv_down_hbm, qkv_up_hbm, w_out_hbm,
+    out_down_hbm, cosine_hbm, sine_hbm,
+    attn_in_ref, low_q_ref, head_ref, base_ref, low_ref,
+    tokens_s, gain_s, w_qkv_s, qkv_down_s, qkv_up_s, w_out_s, out_down_s, cosine_s, sine_s,
+    q_s, k_s, v_s, sem,
+):
+    sources = (
+        tokens_hbm, gain_hbm, qkv_down_hbm, w_qkv_hbm, qkv_up_hbm, cosine_hbm, sine_hbm,
+        w_out_hbm, out_down_hbm,
+    )
+    targets = (
+        tokens_s, gain_s, qkv_down_s, w_qkv_s, qkv_up_s, cosine_s, sine_s, w_out_s, out_down_s,
+    )
+    copies = [
+        pltpu.make_async_copy(source, target, sem.at[number])
+        for number, (source, target) in enumerate(zip(sources, targets))
+    ]
+    for copy in copies:
+        copy.start()
+    rows = tokens_s.shape[0]
+    groups = k_s.shape[0]
+    mask = adapter_mask(length_ref, index_ref, rows, LANES)
+    first = first_keys(length_ref, rows)
+    copies[0].wait()
+    copies[1].wait()
+    inputs = tokens_s[...].astype(F32)
+    inv_root = lax.rsqrt(jnp.mean(inputs * inputs, axis=1, keepdims=True) + EPS)
+    attn_in_ref[...] = (inputs * inv_root * gain_s[...]).astype(BF16)
+    attn_in = attn_in_ref[...]
+    copies[2].wait()
+    low_q = (dot(attn_in, qkv_down_s[...]) * mask).astype(BF16)
+    low_q_ref[...] = low_q
+    for copy in copies[3:7]:
+        copy.wait()
+    projected = dot(attn_in, w_qkv_s[...]) + dot(low_q, qkv_up_s[...])
+    columns = turn(projected, cosine_s[...], sine_s[...], turned_pieces(groups))
+    store_heads(columns, 0, q_s, k_s, v_s)
+    for block in range(rows // ROWS):
+        here = slice(block * ROWS, (block + 1) * ROWS)
+        keys = (block + 1) * ROWS
+        seen = seen_block(first, block)
+        heads = []
+        for group in range(groups):
+            scores = jnp.where(seen, dot_nt(q_s[group, block], k_s[group, :keys, :]), -1e30)
+            lifted = jnp.exp(scores - jnp.max(scores, axis=1, keepdims=True))
+            probs = (lifted * (1.0 / jnp.sum(lifted, axis=1, keepdims=True))).astype(BF16)
+            out = dot(probs, v_s[group, :keys, :])
+            heads += [out[head * ROWS : (head + 1) * ROWS] for head in range(PER)]
+        head_ref[here, :] = jnp.concatenate(heads, axis=1).astype(BF16)
+    copies[7].wait()
+    copies[8].wait()
+    head_out = head_ref[...]
+    base_ref[...] = dot(head_out, w_out_s[...]).astype(BF16)
+    low_ref[...] = (dot(head_out, out_down_s[...]) * mask).astype(BF16)
+
+
+def forward(lengths, index, tokens, gain, w_qkv, qkv_down, qkv_up, w_out, out_down, tables):
+    rows = tokens.shape[0]
+    heads_wide = w_out.shape[0]
+    groups = w_qkv.shape[1] // (HD * (PER + 2))
+    blocks = rows // ROWS
+    arrays = (tokens, gain.reshape(1, D), w_qkv, qkv_down, qkv_up, w_out, out_down) + tables
+    return pl.pallas_call(
+        forward_kernel,
+        in_specs=[IN_SMEM] * 2 + [IN_HBM] * len(arrays),
+        out_specs=[IN_VMEM] * 5,
+        out_shape=[
+            shape((rows, D), BF16),
+            shape((rows, LANES), BF16),
+            shape((rows, heads_wide), BF16),
+            shape((rows, D), BF16),
+            shape((rows, LANES), BF16),
+        ],
+        scratch_shapes=[pltpu.VMEM(array.shape, array.dtype) for array in arrays]
+        + [
+            pltpu.VMEM((groups, blocks, PER * ROWS, HD), BF16),
+            pltpu.VMEM((groups, rows, HD), BF16),
+            pltpu.VMEM((groups, rows, HD), BF16),
+            pltpu.SemaphoreType.DMA((len(arrays),)),
+        ],
+        compiler_params=pltpu.CompilerParams(vmem_limit_bytes=48 * MIB),
+        name="attention_forward",
+    )(lengths, index, *arrays)
+
+
+def experts_kernel(
+    count, tokens_ref, base_ref, low_o_ref, out_up_ref, gain_ref, router_ref, routes_ref, cot_ref,
+    weight_ref, residual_ref, moe_ref, grad_ref,
+    normed_s, gates_s, part_s, moe_s, grad_s,
+):
+    step = pl.program_id(0)
+    lane = lax.broadcasted_iota(jnp.int32, gates_s.shape, 1)
+    width = weight_ref.shape[2] // 3
+
+    @pl.when(step == 0)
+    def _():
+        residual = (
+            tokens_ref[...].astype(F32)
+            + base_ref[...].astype(F32)
+            + dot(low_o_ref[...], out_up_ref[...])
+        )
+        residual_ref[...] = residual
+        inv_root = lax.rsqrt(jnp.mean(residual * residual, axis=1, keepdims=True) + EPS)
+        normed = (residual * inv_root * gain_ref[...]).astype(BF16)
+        normed_s[...] = normed
+        logits = dot(normed, router_ref[...])
+        routed = lane == routes_ref[:, 0:1]
+        for slot in range(1, TOP):
+            routed = routed | (lane == routes_ref[:, slot : slot + 1])
+        logits = jnp.where(routed, logits, -1e30)
+        lifted = jnp.exp(logits - jnp.max(logits, axis=1, keepdims=True))
+        gates_s[...] = lifted / jnp.sum(lifted, axis=1, keepdims=True)
+        part_s[...] = jnp.zeros_like(part_s)
+        moe_s[...] = jnp.zeros_like(moe_s)
+        grad_s[...] = jnp.zeros_like(grad_s)
+
+    normed = normed_s[...]
+    cot = cot_ref[...]
+    gates = gates_s[...]
+    part = jnp.zeros(gates.shape, F32)
+    downs = [
+        jnp.concatenate(
+            [
+                weight_ref[expert, at * LANES : (at + 1) * LANES, 2 * width :]
+                for at in range(D // LANES)
+            ],
+            axis=1,
+        )
+        for expert in range(count)
+    ]
+    hidden, grads = [], []
+    for pair in range(count // 2):
+        both_down = jnp.concatenate(downs[2 * pair : 2 * pair + 2], axis=0)
+        both_raw = dot_nt(cot, both_down)
+        for half in range(2):
+            expert = 2 * pair + half
+            joined = dot(normed, weight_ref[expert, :, : 2 * width])
+            pre_gate = joined[:, :width]
+            pre_up = joined[:, width:]
+            raw = both_raw[:, half * width : (half + 1) * width]
+            sigmoid = 0.5 * jnp.tanh(0.5 * pre_gate) + 0.5
+            activated = pre_gate * sigmoid
+            value = activated * pre_up
+            here = lane == step * count + expert
+            gate = jnp.sum(jnp.where(here, gates, 0.0), axis=1, keepdims=True)
+            part += jnp.where(here, jnp.sum(value * raw, axis=1, keepdims=True), 0.0)
+            hidden.append((gate * value).astype(BF16))
+            inner = raw * gate
+            grads.append((inner * pre_up * (sigmoid + activated * (1.0 - sigmoid))).astype(BF16))
+            grads.append((inner * activated).astype(BF16))
+    part_s[...] += part
+    moe_s[...] += dot(jnp.concatenate(hidden, axis=1), jnp.concatenate(downs, axis=0))
+    ups = jnp.concatenate([weight_ref[expert, :, : 2 * width] for expert in range(count)], axis=1)
+    grad_s[...] += dot_nt(jnp.concatenate(grads, axis=1), ups)
+
+    @pl.when(step == pl.num_programs(0) - 1)
+    def _():
+        gate_part = part_s[...]
+        spread = jnp.sum(gates * gate_part, axis=1, keepdims=True)
+        logit_grad = (gates * (gate_part - spread)).astype(BF16)
+        moe_ref[...] = moe_s[...].astype(BF16)
+        grad_ref[...] = (grad_s[...] + dot_nt(logit_grad, router_ref[...])).astype(BF16)
+
+
+def experts_both(tokens, base, low_o, out_up, gain, router, routes, cot, weights, count=4):
+    rows = tokens.shape[0]
+    experts = weights.shape[0]
+    arrays = (tokens, base, low_o, out_up, gain.reshape(1, D), router, routes, cot)
+    whole = pl.BlockSpec((rows, D), lambda step: (0, 0))
+    return pl.pallas_call(
+        functools.partial(experts_kernel, count),
+        grid=(experts // count,),
+        in_specs=[pl.BlockSpec(array.shape, lambda step: (0, 0)) for array in arrays]
+        + [pl.BlockSpec((count,) + weights.shape[1:], lambda step: (step, 0, 0))],
+        out_specs=[whole] * 3,
+        out_shape=[shape((rows, D), F32), shape((rows, D), BF16), shape((rows, D), BF16)],
+        scratch_shapes=[
+            pltpu.VMEM((rows, D), BF16),
+            pltpu.VMEM((rows, experts), F32),
+            pltpu.VMEM((rows, experts), F32),
+            pltpu.VMEM((rows, D), F32),
+            pltpu.VMEM((rows, D), F32),
+        ],
+        compiler_params=pltpu.CompilerParams(vmem_limit_bytes=60 * MIB),
+        name="experts",
+    )(*arrays, weights)
+
+
+def norm_back(vectors, gain, upstream):
+    inv_root = lax.rsqrt(jnp.mean(vectors * vectors, axis=1, keepdims=True) + EPS)
+    weighted = upstream * gain
+    slope = jnp.mean(vectors * weighted, axis=1, keepdims=True)
+    return inv_root * weighted - vectors * (inv_root * inv_root * inv_root) * slope
+
+
+def branch_kernel(
+    length_ref, index_ref, residual_ref, low_o_ref, normed_grad_ref, cot_ref, gain_ref, out_up_ref,
+    head_ref, shares, residual_grad_ref, head_grad_ref, part_ref, w_out_s, sem,
+):
+    n_exp, n_tp, _, wide = shares.shape
+    rows = residual_ref.shape[0]
+    qkv_rows, up_rows, out_rows = share_rows(n_exp, w_out_s.shape[1])
+    copies = []
+    for z in range(n_tp):
+        for e in range(n_exp):
+            at = qkv_rows + up_rows
+            for left in range(0, D, wide):
+                taken = min(wide, D + LANES - left)
+                copies.append(
+                    pltpu.make_async_copy(
+                        shares.at[e, z, at : at + out_rows, :taken],
+                        w_out_s.at[z, e * out_rows : (e + 1) * out_rows, left : left + taken],
+                        sem.at[len(copies)],
+                    )
+                )
+                at += out_rows
+    for copy in copies:
+        copy.start()
+    mask = adapter_mask(length_ref, index_ref, rows, LANES)
+    low_o = low_o_ref[...]
+    residual_grad_ref[...] = cot_ref[...].astype(F32) + norm_back(
+        residual_ref[...], gain_ref[...], normed_grad_ref[...].astype(F32)
+    )
+    branch_grad = residual_grad_ref[...].astype(BF16)
+    low_o_grad = (dot_nt(branch_grad, out_up_ref[...]) * mask).astype(BF16)
+    for at in range(D // LANES):
+        lanes = slice(at * LANES, (at + 1) * LANES)
+        part_ref[lanes, :] = dot_tn(low_o, branch_grad[:, lanes]).astype(BF16)
+    part_ref[D:, :] = dot_tn(head_ref[...], low_o_grad).astype(BF16)
+    for copy in copies:
+        copy.wait()
+    for z in range(n_tp):
+        head_grad_ref[z] = (
+            dot_nt(branch_grad, w_out_s[z, :, :D]) + dot_nt(low_o_grad, w_out_s[z, :, D:])
+        ).astype(BF16)
+
+
+def branch_back(lengths, index, residual, low_o, normed_grad, cot, gain, out_up, head, shares):
+    rows, heads_wide = head.shape
+    n_exp, n_tp, _, wide = shares.shape
+    return pl.pallas_call(
+        branch_kernel,
+        in_specs=[IN_SMEM] * 2 + [IN_VMEM] * 7 + [IN_HBM],
+        out_specs=[IN_VMEM] * 3,
+        out_shape=[
+            shape((rows, D), F32),
+            shape((n_tp, rows, heads_wide), BF16),
+            shape((D + heads_wide, LANES), BF16),
+        ],
+        scratch_shapes=[
+            pltpu.VMEM((n_tp, heads_wide, D + LANES), BF16),
+            pltpu.SemaphoreType.DMA((n_tp * n_exp * -(-D // wide),)),
+        ],
+        compiler_params=pltpu.CompilerParams(vmem_limit_bytes=48 * MIB),
+        name="branch_backward",
+    )(
+        lengths, index, residual, low_o, normed_grad, cot, gain.reshape(1, D), out_up, head, shares
+    )
+
+
+def backward_kernel(
+    place_ref, length_ref, index_ref, attn_in_ref, low_q_ref, head_grad_ref, residual_grad_ref,
+    tokens_ref, gain_ref, qkv_down_ref, cosine_ref, sine_ref, shares,
+    input_grad_ref, part_ref,
+    w_qkv_s, q_s, k_s, v_s, g_s, grad_s, sum_s, sem,
+):
+    n_exp, n_tp, _, wide = shares.shape
+    rows = tokens_ref.shape[0]
+    blocks = rows // ROWS
+    groups = k_s.shape[0] // n_tp
+    flags = turned_pieces(groups)
+    scale = 1.0 / math.sqrt(HD)
+    qkv_rows, up_rows, _ = share_rows(n_exp, 0)
+    copies = []
+    for z in range(n_tp):
+        for e in range(n_exp):
+            for source, target in (
+                (shares.at[e, z, :qkv_rows, :], pl.ds(e * qkv_rows, qkv_rows)),
+                (
+                    shares.at[e, z, qkv_rows : qkv_rows + up_rows, :],
+                    pl.ds(D + e * up_rows, up_rows),
+                ),
+            ):
+                copies.append(
+                    pltpu.make_async_copy(source, w_qkv_s.at[z, target, :], sem.at[len(copies)])
+                )
+    for copy in copies:
+        copy.start()
+    first = first_keys(length_ref, rows)
+    attn_in = attn_in_ref[...]
+    low_q = low_q_ref[...]
+    seen = [seen_block(first, block) for block in range(blocks)]
+    for z in range(n_tp):
+        for copy in copies[z * 2 * n_exp : (z + 1) * 2 * n_exp]:
+            copy.wait()
+        projected = dot(attn_in, w_qkv_s[z, :D, :]) + dot(low_q, w_qkv_s[z, D:, :])
+        columns = turn(projected, cosine_ref[...], sine_ref[...], flags)
+        store_heads(columns, z * groups, q_s, k_s, v_s)
+        for head in range(groups * PER):
+            group, kind = divmod(head, PER)
+            part = head_grad_ref[z, :, head * HD : (head + 1) * HD]
+            for block in range(blocks):
+                g_s[z * groups + group, block, kind * ROWS : (kind + 1) * ROWS, :] = part[
+                    block * ROWS : (block + 1) * ROWS
+                ]
+
+    def one_place(z, carried):
+        pieces = []
+        for group in range(groups):
+            at = z * groups + group
+            key_grad = jnp.zeros((HD, rows), F32)
+            value_grad = jnp.zeros((HD, rows), F32)
+            query_grads = []
+            for block in range(blocks):
+                count = (block + 1) * ROWS
+                query, grad = q_s[at, block], g_s[at, block]
+                key, value = k_s[at, :count, :], v_s[at, :count, :]
+                scores = jnp.where(seen[block], dot_nt(query, key), -1e30)
+                lifted = jnp.exp(scores - jnp.max(scores, axis=1, keepdims=True))
+                probs = lifted * (1.0 / jnp.sum(lifted, axis=1, keepdims=True))
+                weight_grad = dot_nt(grad, value)
+                spread = jnp.sum(probs * weight_grad, axis=1, keepdims=True)
+                score_grad = (probs * (weight_grad - spread)).astype(BF16)
+                query_grads.append(dot(score_grad, key) * scale)
+
+                def widen(part):
+                    if count == rows:
+                        return part
+                    return jnp.concatenate([part, jnp.zeros((HD, rows - count), F32)], axis=1)
+
+                key_grad += widen(dot_tn(query, score_grad))
+                value_grad += widen(dot_tn(grad, probs.astype(BF16)))
+            for head in range(PER):
+                here = slice(head * ROWS, (head + 1) * ROWS)
+                pieces.append(jnp.concatenate([part[here] for part in query_grads], axis=0))
+            pieces += [key_grad.T, value_grad.T]
+        joined = jnp.concatenate(pieces, axis=1)
+        columns = turn(joined, cosine_ref[...], -sine_ref[...], flags)
+        for at, column in enumerate(columns):
+            grad_s[z, :, at * LANES : (at + 1) * LANES] = column.astype(BF16)
+        return carried
+
+    lax.fori_loop(0, n_tp, one_place, 0)
+    sum_s[...] = dot_nt(grad_s[0], w_qkv_s[0])
+    for z in range(1, n_tp):
+        sum_s[...] += dot_nt(grad_s[z], w_qkv_s[z])
+    mask = adapter_mask(length_ref, index_ref, rows, LANES)
+    low_q_grad = (sum_s[:, D:] * mask).astype(BF16)
+    part_ref[:D, :] = dot_tn(attn_in, low_q_grad).astype(BF16)
+    own = grad_s[place_ref[0]]
+    for at in range(wide // LANES):
+        lanes = slice(at * LANES, (at + 1) * LANES)
+        part_ref[D + at * LANES : D + (at + 1) * LANES, :] = dot_tn(low_q, own[:, lanes]).astype(
+            BF16
+        )
+    attn_grad = sum_s[:, :D] + dot_nt(low_q_grad, qkv_down_ref[...])
+    input_grad_ref[...] = (
+        residual_grad_ref[...]
+        + norm_back(tokens_ref[...].astype(F32), gain_ref[...], attn_grad)
+    ).astype(BF16)
+
+
+def attention_back(
+    place, lengths, index, attn_in, low_q, head_grad, residual_grad, tokens, gain, qkv_down, tables,
+    shares,
+):
+    rows = tokens.shape[0]
+    n_exp, n_tp, _, wide = shares.shape
+    count = KV_HEADS
+    blocks = rows // ROWS
+    arrays = (attn_in, low_q, head_grad, residual_grad, tokens, gain.reshape(1, D), qkv_down)
+    return pl.pallas_call(
+        backward_kernel,
+        in_specs=[IN_SMEM] * 3 + [IN_VMEM] * 9 + [IN_HBM],
+        out_specs=[IN_VMEM] * 2,
+        out_shape=[shape((rows, D), BF16), shape((D + wide, LANES), BF16)],
+        scratch_shapes=[
+            pltpu.VMEM((n_tp, D + LANES, wide), BF16),
+            pltpu.VMEM((count, blocks, PER * ROWS, HD), BF16),
+            pltpu.VMEM((count, rows, HD), BF16),
+            pltpu.VMEM((count, rows, HD), BF16),
+            pltpu.VMEM((count, blocks, PER * ROWS, HD), BF16),
+            pltpu.VMEM((n_tp, rows, wide), BF16),
+            pltpu.VMEM((rows, D + LANES), F32),
+            pltpu.SemaphoreType.DMA((n_tp * n_exp * 2,)),
+        ],
+        compiler_params=pltpu.CompilerParams(vmem_limit_bytes=60 * MIB),
+        name="attention_backward",
+    )(place, lengths, index, *arrays, *tables, shares)
+
+
+def kernel_body(
+    tokens, attn_gain, moe_gain, w_qkv, w_out, w_router, w_gate, w_up, w_down, qkv_down, qkv_up,
+    out_down, out_up, lengths, adapter_index, loss_mask, routes, upstream,
+):
+    n_exp = lax.axis_size("exp")
+    rows = tokens.shape[0]
+    heads_wide = w_out.shape[0]
+    wide = w_qkv.shape[1]
+    exp_place = lax.axis_index("exp").astype(jnp.int32).reshape(1)
+    tp_place = lax.axis_index("tp").astype(jnp.int32).reshape(1)
+    tables = turn_tables(rows)
+    own_experts, own_shares = pack(
+        exp_place, w_gate, w_up, w_down, w_qkv, qkv_up, w_out, out_down, n_exp
+    )
+    weights = lax.all_gather(own_experts, "exp", axis=0, tiled=True)
+    attn_in, low_q, head, base, low_o = forward(
+        lengths, adapter_index, tokens, attn_gain, w_qkv, qkv_down, qkv_up, w_out, out_down, tables
+    )
+    base, low_o = lax.psum((base, low_o), "tp")
+    own_shares, _ = lax.optimization_barrier((own_shares, base))
+    shares = lax.all_gather(own_shares, "tp", axis=0)
+    shares, _ = lax.optimization_barrier((shares, weights))
+    shares = lax.all_gather(shares, "exp", axis=0)
+    occupied = jnp.arange(rows, dtype=jnp.int32) < jnp.sum(lengths)
+    kept = occupied & (loss_mask > 0)
+    cot = jnp.where(kept[:, None], upstream, jnp.zeros((), BF16))
+    residual, moe_part, normed_part = experts_both(
+        tokens, base, low_o, out_up, moe_gain, w_router, routes, cot, weights
+    )
+    normed_grad = lax.psum(normed_part, "tp")
+    moe_part, _ = lax.optimization_barrier((moe_part, normed_grad))
+    moe_out = lax.psum(moe_part, "tp").astype(F32)
+    output = (residual + moe_out).astype(BF16)
+    residual_grad, head_grad, out_part = branch_back(
+        lengths, adapter_index, residual, low_o, normed_grad, cot, moe_gain, out_up, head, shares
+    )
+    input_grad, qkv_part = attention_back(
+        tp_place, lengths, adapter_index, attn_in, low_q, head_grad, residual_grad, tokens,
+        attn_gain, qkv_down, tables, shares,
+    )
+    parts = jnp.concatenate([out_part, qkv_part], axis=0)
+    share = parts.shape[0] // n_exp
+    parts = lax.all_to_all(parts.reshape(n_exp, share, LANES), "exp", 0, 0, tiled=True)
+    summed = jnp.sum(parts.astype(F32), axis=0).astype(BF16)
+    summed = lax.all_gather(summed, "exp", axis=0, tiled=True).astype(F32)
+
+    def side_by_side(stacked):
+        pieces = stacked.reshape(-1, LANES, LANES)
+        return pieces.transpose(1, 0, 2).reshape(LANES, -1)
+
+    at = D + heads_wide
+    return (
+        output,
+        input_grad,
+        summed[at : at + D],
+        side_by_side(summed[at + D :]),
+        summed[D:at],
+        side_by_side(summed[:D]),
+    )
 
 
 def product(left_m, right_m):
@@ -255,6 +880,12 @@
     return (output, input_grad, summed[0], summed[1], summed[2], summed[3])
 
 
+def kernels_fit(mesh):
+    n_exp, n_tp = mesh.shape["exp"], mesh.shape["tp"]
+    groups = KV_HEADS // n_tp
+    return groups % 2 == 0 and FF // n_tp == LANES and LANES // n_exp % 16 == 0
+
+
 def solution(mesh):
     placed = (
         P("exp", None),
@@ -277,7 +908,7 @@
         P("exp", None),
     )
     return jax.shard_map(
-        body,
+        kernel_body if kernels_fit(mesh) else body,
         mesh=mesh,
         in_specs=placed,
         out_specs=(P("exp", None), P("exp", None), P(), P(None, "tp"), P("tp", None), P()),

time: 488 us -> 469 us (0.961)
  Pallas kernels: 0 us -> 188 us
  waiting for transfers between devices: 329 us -> 208 us
  matrix products: 84.2 us -> 0 us
  other arithmetic: 38.4 us -> 8.79 us
  blocking collectives: 0 us -> 18.7 us
  local copies, waits for them, and re-layouts: 11.6 us -> 21.2 us
    psum x4 -> x3, waiting for transfers between devices: 299 us -> 59.8 us  [the longest x1 59.7 us: kernel_body(): normed_grad = lax.psum(normed_part, 'tp')]
    pallas_call x0 -> x5, Pallas kernels: none -> 188 us  [the longest x1 85.8 us: pack(): pl.pallas_call(functools.partial(pack_kernel, n_exp), in_specs=[IN_SMEM]...]
    all_gather x2 -> x4, waiting for transfers between devices: 29.8 us -> 148 us  [the longest x1 95.5 us: kernel_body(): weights = lax.all_gather(own_experts, 'exp', axis=0, tiled=True)]
    dot_general x28 -> x0, matrix products: 84.2 us -> none  [the longest x17 69.6 us: contract(): jnp.einsum(einsum_form, left_m, right_m, preferred_element_type=jnp.float32)]
    all_to_all x0 -> x1, blocking collectives: none -> 18.7 us  [kernel_body(): lax.all_to_all(parts.reshape(n_exp, share, LANES), 'exp', 0, 0, tiled=True)]
    convert_element_type x7 -> x1, other arithmetic: 16.3 us -> 3.01 us  [kernel_body(): output = (residual + moe_out).astype(BF16)]
    unnamed x124 -> x60, local copies, waits for them, and re-layouts: 6.92 us -> 16.8 us
    another operation x6 -> x0, other arithmetic: 5.04 us -> none
  transfers between devices with their start and end apart: 6 -> 7, of which waited for: 5 -> 5; matrix products, arithmetic and copies ran while one was open for 9% -> 2% of each run, Pallas kernels for 0% -> 38%
where the time goes in v2:
time: 469 us; the launch traced here: 462 us
  waiting for transfers between devices  208 us (44%)
  Pallas kernels  188 us (40%)
  local copies, waits for them, and re-layouts  21.2 us (5%)
  blocking collectives  18.7 us (4%)
  between operations  15.9 us (3%)
  other arithmetic  8.79 us (2%)
    all_gather x1, waiting for transfers between devices, kernel_body(): weights = lax.all_gather(own_experts, 'exp', axis=0, tiled=True)  95.5 us
    pallas_call x1, Pallas kernels, pack(): pl.pallas_call(functools.partial(pack_kernel, n_exp), in_specs=[IN_SMEM]...  85.8 us
    psum x1, waiting for transfers between devices, kernel_body(): normed_grad = lax.psum(normed_part, 'tp')  59.7 us
    pallas_call x1, Pallas kernels, attention_back(): pl.pallas_call(backward_kernel, in_specs=[IN_SMEM] * 3 + [IN_VMEM] * 9 +...  49.7 us
    pallas_call x1, Pallas kernels, experts_both(): pl.pallas_call(functools.partial(experts_kernel, count), grid=(experts //...  30.4 us
    all_gather x1, waiting for transfers between devices, kernel_body(): shares = lax.all_gather(shares, 'exp', axis=0)  20.2 us
    all_gather x1, waiting for transfers between devices, kernel_body(): summed = lax.all_gather(summed, 'exp', axis=0, tiled=True).astype(F32)  19.5 us
    all_to_all x1, blocking collectives, kernel_body(): lax.all_to_all(parts.reshape(n_exp, share, LANES), 'exp', 0, 0, tiled=True)  18.7 us
  transfers between devices with their start and end apart: 7, of which 5 were waited for; matrix products, arithmetic and copies ran while one was open for 2% of the time, Pallas kernels for 38%

profile of v2, /device:TPU:0, one launch (start us, length us, event | category | flops | bytes accessed | tf_op | source)
XLA Modules:
  0.0 461.9 jit_solution(12830526364107437248)
XLA Ops:
  8.0 0.0 all-reduce.9.cloned.1.call-start
  8.0 0.7 reshape.42.gain_hbm.gain_ref
  8.7 1.3 copy-done.1
  10.0 1.0 copy-done.6
  11.0 0.9 copy-done.7
  12.0 0.9 copy-done.8
  12.9 0.9 copy-done.9
  13.8 0.9 copy-done.13
  14.7 0.7 copy-done.17
  15.4 0.7 copy-done.19
  16.0 11.4 %attention_forward.1 = (bf16[512,1536]{1,0:T(8,128)(2,1)S(1)}, bf16[512,128]{1,0:T(8,128)(2,1)S(1)}, bf16[512,384]{1,0:T(8,128)(2,1)S(1)}, bf16[512,1536]{1,0:T(8,128)(2,1)}, bf16[512,128]{1,0:T(8,128)(2,1)}) custom-call(s32[1,4]{1,0:T(1,128)S(1)} %copy-done.17, s32[1,4]{1,0:T(1,128)S(1)} %copy-done.19, bf16[512,1536]{1,0:T(8,128)(2,1)} %tokens_ref.3, ...), custom_call_target="tpu_custom_call" | custom-call | tf_op jit(solution)/shard_map/attention_forward/pallas_call | solution.py:259
  27.4 1.2 copy-done.2
  28.7 0.7 copy-done.11
  29.4 0.7 copy-done.14
  30.1 0.0 all-reduce.9.cloned.1.call-update
  30.1 0.0 all-gather.7.cloned.1.call-start
  30.1 85.8 %pack_weights.1 = (bf16[2,1536,384]{2,1,0:T(8,128)(2,1)}, bf16[352,640]{1,0:T(8,128)(2,1)}) custom-call(s32[1]{0:T(128)} %bitcast.place_ref, bf16[2,1536,128]{2,1,0:T(8,128)(2,1)} %gate.1, bf16[2,1536,128]{2,1,0:T(8,128)(2,1)} %up.1, bf16[2,128,1536]{2,1,0:T(8,128)(2,1)} %down.1, bf16[1536,640]{1,0:T(8,128)(2,1)} %w_qkv.1, bf16[128,640]{1,0:T(8,128)(2,1)} %qkv_up.1, ...), custom_call_target="tpu_custom_call" | custom-call | tf_op jit(solution)/shard_map/pack_weights/pallas_call | solution.py:183
  115.9 0.0 copy-start.26
  115.9 0.0 copy-start.24
  116.0 0.0 copy-start.25
  116.0 0.0 copy-start.18
  116.0 0.0 copy-start.27
  116.0 0.0 copy-start.23
  116.0 0.0 all-gather.7.cloned.1.call-update
  116.0 0.0 all-gather.11.cloned.1.call-start
  116.1 0.0 all-reduce.9.cloned.1.call-done
  116.1 0.5 all-gather.11.cloned.1.call-update
  116.6 0.2 all-reduce.5.cloned.1.call-start
  116.9 0.6 reshape.43.gain_ref
  117.5 0.9 copy.40.router_ref
  118.4 0.8 copy.41.routes_ref
  119.3 0.6 reduce_sum.21
  119.9 0.7 fusion
  120.6 1.3 broadcast_select_fusion.cot_ref
  121.9 95.5 %all-gather.7.cloned.1.call-done.weight_ref = bf16[16,1536,384]{2,1,0:T(8,128)(2,1)} async-done(((bf16[2,1536,384]{2,1,0:T(8,128)(2,1)}), bf16[16,1536,384]{2,1,0:T(8,128)(2,1)}) %all-gather.7.cloned.1.call-update) | async-done | bytes 18874384 | tf_op jit(solution)/shard_map/all_gather | solution.py:602
  217.4 30.4 %experts.1 = (f32[512,1536]{1,0:T(8,128)}, bf16[512,1536]{1,0:T(8,128)(2,1)}, bf16[512,1536]{1,0:T(8,128)(2,1)}) custom-call(bf16[512,1536]{1,0:T(8,128)(2,1)} %tokens_ref.3, bf16[512,1536]{1,0:T(8,128)(2,1)} %get-tuple-element.60.base_ref, bf16[512,128]{1,0:T(8,128)(2,1)} %get-tuple-element.61.low_o_ref, bf16[128,1536]{1,0:T(8,128)(2,1)} %out_up_ref.3, ...), custom_call_target="tpu_custom_call" | custom-call | tf_op jit(solution)/shard_map/experts/pallas_call | solution.py:366
  247.8 0.0 all-reduce.5.cloned.1.call-update
  247.8 0.0 all-gather.13.cloned.1.call-start
  247.9 12.7 %all-gather.11.cloned.1.call-done = bf16[1408,640]{1,0:T(8,128)(2,1)} async-done(((bf16[352,640]{1,0:T(8,128)(2,1)}), bf16[1408,640]{1,0:T(8,128)(2,1)}) %all-gather.11.cloned.1.call-update) | async-done | bytes 1802256 | tf_op jit(solution)/shard_map/all_gather | solution.py:608
  260.6 0.0 all-gather.13.cloned.1.call-update
  260.6 0.0 all-reduce.7.cloned.1.call-start
  260.6 59.7 %all-reduce.5.cloned.1.call-done.normed_grad_ref = bf16[512,1536]{1,0:T(8,128)(2,1)} async-done(((bf16[512,1536]{1,0:T(8,128)(2,1)}), bf16[512,1536]{1,0:T(8,128)(2,1)}) %all-reduce.5.cloned.1.call-update) | async-done | bytes 1572880 | tf_op jit(solution)/shard_map/psum | solution.py:617
  320.4 0.0 all-reduce.7.cloned.1.call-update
  320.4 0.3 all-gather.9.cloned.1.call-start
  320.7 20.2 %all-gather.13.cloned.1.call-done = bf16[32,352,640]{2,1,0:T(8,128)(2,1)} async-done(((bf16[4,352,640]{2,1,0:T(8,128)(2,1)}), bf16[32,352,640]{2,1,0:T(8,128)(2,1)}) %all-gather.13.cloned.1.call-update) | async-done | bytes 14417936 | tf_op jit(solution)/shard_map/all_gather | solution.py:610
  340.9 0.9 copy-done.10
  341.8 1.0 copy-done.12
  342.8 11.0 %branch_backward.1 = (f32[512,1536]{1,0:T(8,128)}, bf16[4,512,384]{2,1,0:T(8,128)(2,1)S(1)}, bf16[1920,128]{1,0:T(8,128)(2,1)S(1)}) custom-call(s32[1,4]{1,0:T(1,128)S(1)} %copy-done.18, s32[1,4]{1,0:T(1,128)S(1)} %copy-done.20, f32[512,1536]{1,0:T(8,128)} %get-tuple-element.27.residual_ref, bf16[512,128]{1,0:T(8,128)(2,1)S(1)} %copy-done.10, ...), custom_call_target="tpu_custom_call" | custom-call | tf_op jit(solution)/shard_map/branch_backward/pallas_call | solution.py:437
  353.8 1.1 copy-done.4
  355.0 49.7 %attention_backward.1 = (bf16[512,1536]{1,0:T(8,128)(2,1)}, bf16[2176,128]{1,0:T(8,128)(2,1)}) custom-call(s32[1]{0:T(128)} %bitcast.1.place_ref, s32[1,4]{1,0:T(1,128)} %length_ref.5, s32[1,4]{1,0:T(1,128)} %index_ref.5, bf16[512,1536]{1,0:T(8,128)(2,1)} %copy-done.2, bf16[512,128]{1,0:T(8,128)(2,1)} %copy-done.14, bf16[4,512,384]{2,1,0:T(8,128)(2,1)} %copy-done.4, ...), custom_call_target="tpu_custom_call" | custom-call | tf_op jit(solution)/shard_map/attention_backward/pallas_call | solution.py:568
  404.7 1.1 pad_maximum_fusion
  405.8 18.7 %all_to_all.5 = bf16[8,512,128]{2,1,0:T(8,128)(2,1)} all-to-all(bf16[8,512,128]{2,1,0:T(8,128)(2,1)S(1)} %bitcast.15), channel_id=1, replica_groups=mesh['exp'=8,'tp'=4] {'exp'}, dimensions={0} | all-to-all | bytes 2097152 | tf_op jit(solution)/shard_map/all_to_all | solution.py:630
  424.6 2.1 reduce_sum.22
  426.6 0.0 all-gather.9.cloned.1.call-update
  426.6 0.0 all-reduce.7.cloned.1.call-done
  426.7 3.0 add_convert_fusion
  429.7 19.5 %all-gather.9.cloned.1.call-done = bf16[4096,128]{1,0:T(8,128)(2,1)} async-done(((bf16[512,128]{1,0:T(8,128)(2,1)}), bf16[4096,128]{1,0:T(8,128)(2,1)}) %all-gather.9.cloned.1.call-update) | async-done | bytes 1048592 | tf_op jit(solution)/shard_map/all_gather | solution.py:632
  449.1 1.0 slice.17
  450.2 0.2 copy.42
  450.3 0.9 copy.44
  451.2 1.0 fusion.1
  452.2 0.3 copy.43
  452.5 1.1 copy.45
  453.6 0.7 slice.18
  (36 shorter events, 0.1 us)
Async XLA Ops:
  8.0 108.1 %all-reduce.9.cloned.1.call-start = ((), (), s32[]{:S(2)}) async-start(), calls=%async_computation.7 | async-start | bytes 3407872 | tf_op jit(solution)/shard_map/psum | solution.py:606
  8.7 1.3 copy-start.1
  10.0 1.0 copy-start.6
  11.0 0.9 copy-start.7
  12.0 0.9 copy-start.8
  12.9 0.9 copy-start.9
  13.8 0.9 copy-start.13
  14.7 0.7 copy-start.17
  15.4 0.7 copy-start.19
  16.0 11.4 %copy-start.16 = (f32[1,1536]{1,0:T(1,128)}, f32[1,1536]{1,0:T(1,128)S(1)}, u32[]{:S(2)}) copy-start(f32[1,1536]{1,0:T(1,128)S(1)} %reshape.42.gain_hbm.gain_ref) | copy-start | bytes 18436
  27.4 1.2 copy-start.2
  28.7 0.7 copy-start.11
  29.4 0.7 copy-start.14
  30.1 187.3 %all-gather.7.cloned.1.call-start = ((), (), s32[]{:S(2)}) async-start(), calls=%async_computation.1 | async-start | bytes 21233664 | tf_op jit(solution)/shard_map/all_gather | solution.py:602
  115.9 0.9 copy-start.26
  115.9 1.5 copy-start.24
  116.0 2.5 copy-start.25
  116.0 3.3 copy-start.18
  116.0 3.9 copy-start.27
  116.0 4.6 copy-start.23
  116.0 144.5 %all-gather.11.cloned.1.call-start = ((), (), s32[]{:S(2)}) async-start(), calls=%async_computation.5 | async-start | bytes 2252800 | tf_op jit(solution)/shard_map/all_gather | solution.py:608
  116.6 203.7 %all-reduce.5.cloned.1.call-start = ((), (), s32[]{:S(2)}) async-start(), calls=%async_computation.2 | async-start | bytes 3145728 | tf_op jit(solution)/shard_map/psum | solution.py:617
  247.8 93.1 %copy-start.5 = (bf16[128,1536]{1,0:T(8,128)(2,1)S(1)}, bf16[128,1536]{1,0:T(8,128)(2,1)}, u32[]{:S(2)}) copy-start(bf16[128,1536]{1,0:T(8,128)(2,1)} %out_up_ref.3) | copy-start | bytes 1179652
  247.8 93.0 %all-gather.13.cloned.1.call-start = ((), (), s32[]{:S(2)}) async-start(), calls=%async_computation.6 | async-start | bytes 16220160 | tf_op jit(solution)/shard_map/all_gather | solution.py:610
  260.5 80.3 %copy-start = (bf16[512,1536]{1,0:T(8,128)(2,1)S(1)}, bf16[512,1536]{1,0:T(8,128)(2,1)}, u32[]{:S(2)}) copy-start(bf16[512,1536]{1,0:T(8,128)(2,1)} %broadcast_select_fusion.cot_ref) | copy-start | bytes 4718596
  260.5 80.3 %copy-start.15 = (f32[1,1536]{1,0:T(1,128)S(1)}, f32[1,1536]{1,0:T(1,128)}, u32[]{:S(2)}) copy-start(f32[1,1536]{1,0:T(1,128)} %reshape.43.gain_ref) | copy-start | bytes 18436
  260.6 80.3 %copy-start.20 = (s32[1,4]{1,0:T(1,128)S(1)}, s32[1,4]{1,0:T(1,128)}, u32[]{:S(2)}) copy-start(s32[1,4]{1,0:T(1,128)} %index_ref.5) | copy-start | bytes 52
  260.6 166.1 %all-reduce.7.cloned.1.call-start = ((), (), s32[]{:S(2)}) async-start(), calls=%async_computation.3 | async-start | bytes 3145728 | tf_op jit(solution)/shard_map/psum | solution.py:619
  320.4 20.5 %copy-start.3 = (bf16[512,1536]{1,0:T(8,128)(2,1)S(1)}, bf16[512,1536]{1,0:T(8,128)(2,1)}, u32[]{:S(2)}) copy-start(bf16[512,1536]{1,0:T(8,128)(2,1)} %all-reduce.5.cloned.1.call-done.normed_grad_ref) | copy-start | bytes 4718596
  320.4 128.8 %all-gather.9.cloned.1.call-start = ((), (), s32[]{:S(2)}) async-start(), calls=%async_computation.4 | async-start | bytes 1179648 | tf_op jit(solution)/shard_map/all_gather | solution.py:632
  340.9 0.9 copy-start.10
  341.8 1.0 copy-start.12
  353.8 1.2 copy-start.4
  405.8 20.9 %copy-start.21 = (f32[512,1536]{1,0:T(8,128)S(1)}, f32[512,1536]{1,0:T(8,128)}, u32[]{:S(2)}) copy-start(f32[512,1536]{1,0:T(8,128)} %get-tuple-element.27.residual_ref) | copy-start | bytes 9437188
  449.1 2.1 copy-start.22
Sparse Core Ops, SparseCore 0:
  30.2 76.4 all-reduce.8
  248.0 72.3 all-reduce.4
  323.3 68.1 all-reduce.6
Sparse Core Ops, SparseCore 1:
  116.1 101.2 all-gather.6
  219.4 41.1 all-gather.10
  262.3 78.5 all-gather.12
  426.7 22.4 all-gather.8

commit v3 on v2

--- a/solution.py
+++ b/solution.py
@@ -31,9 +31,10 @@
 MIB = 2**20
 NT = (((1,), (1,)), ((), ()))
 TN = (((0,), (0,)), ((), ()))
+WHOLE_VMEM = pltpu.CompilerParams(vmem_limit_bytes=63 * MIB)
 IN_VMEM = pl.BlockSpec(memory_space=pltpu.VMEM)
 IN_SMEM = pl.BlockSpec(memory_space=pltpu.SMEM)
-IN_HBM = pl.BlockSpec(memory_space=pl.ANY)
+IN_HBM = pl.BlockSpec(memory_space=pltpu.HBM)
 
 
 def dot(left, right):
@@ -46,6 +47,10 @@
 
 def dot_tn(left, right):
     return lax.dot_general(left, right, TN, preferred_element_type=F32)
+
+
+def cost(flops, moved):
+    return pl.CostEstimate(flops=int(flops), bytes_accessed=int(moved), transcendentals=0)
 
 
 def shape(dims, dtype):
@@ -133,104 +138,146 @@
                     ]
 
 
-def pack_kernel(
-    n_exp, place_ref, gate, up, down, w_qkv, qkv_up, w_out, out_down, experts, shares, sem
-):
+def run_copies(pairs, sem):
+    copies = [
+        pltpu.make_async_copy(source, target, sem.at[number])
+        for number, (source, target) in enumerate(pairs)
+    ]
+    for copy in copies:
+        copy.start()
+    for copy in copies:
+        copy.wait()
+
+
+def pack_experts_kernel(gate, up, down, packed, held, sem, out_sem):
     width = gate.shape[2]
-    copies = []
+    pairs = []
     for expert in range(gate.shape[0]):
-        copies.append((gate.at[expert], experts.at[expert, :, :width]))
-        copies.append((up.at[expert], experts.at[expert, :, width : 2 * width]))
+        pairs.append((gate.at[expert], held.at[expert, :, :width]))
+        pairs.append((up.at[expert], held.at[expert, :, width : 2 * width]))
         for at in range(D // LANES):
             lanes = slice(at * LANES, (at + 1) * LANES)
-            copies.append((down.at[expert, :, lanes], experts.at[expert, lanes, 2 * width :]))
+            pairs.append((down.at[expert, :, lanes], held.at[expert, lanes, 2 * width :]))
+    run_copies(pairs, sem)
+    run_copies([(held, packed)], out_sem)
+
+
+def pack_experts(w_gate, w_up, w_down):
+    count, _, width = w_gate.shape
+    packed = shape((count, D, 3 * width), BF16)
+    return pl.pallas_call(
+        pack_experts_kernel,
+        in_specs=[IN_HBM] * 3,
+        out_specs=IN_HBM,
+        out_shape=packed,
+        scratch_shapes=[
+            pltpu.VMEM(packed.shape, BF16),
+            pltpu.SemaphoreType.DMA((count * (2 + D // LANES),)),
+            pltpu.SemaphoreType.DMA((1,)),
+        ],
+        compiler_params=WHOLE_VMEM,
+        cost_estimate=cost(0, 2 * 2 * count * D * 3 * width),
+        name="pack_experts",
+    )(w_gate, w_up, w_down)
+
+
+def share_rows(n_exp, heads_wide):
+    return (D // n_exp, LANES // n_exp, heads_wide // n_exp)
+
+
+def pack_share_kernel(n_exp, place_ref, w_qkv, qkv_up, w_out, out_down, packed, held, sem, out_sem):
     qkv_rows, up_rows, out_rows = share_rows(n_exp, w_out.shape[0])
     place = place_ref[0]
     own_qkv = pl.ds(pl.multiple_of(place * qkv_rows, 16), qkv_rows)
     own_up = pl.ds(pl.multiple_of(place * up_rows, 16), up_rows)
     own_out = pl.ds(pl.multiple_of(place * out_rows, 16), out_rows)
     wide = w_qkv.shape[1]
-    copies.append((w_qkv.at[own_qkv, :], shares.at[:qkv_rows, :]))
     at = qkv_rows + up_rows
-    copies.append((qkv_up.at[own_up, :], shares.at[qkv_rows:at, :]))
+    pairs = [
+        (w_qkv.at[own_qkv, :], held.at[:qkv_rows, :]),
+        (qkv_up.at[own_up, :], held.at[qkv_rows:at, :]),
+    ]
     for left in range(0, D, wide):
         taken = min(wide, D - left)
-        target = shares.at[at : at + out_rows, :taken]
-        copies.append((w_out.at[own_out, left : left + taken], target))
+        target = held.at[at : at + out_rows, :taken]
+        pairs.append((w_out.at[own_out, left : left + taken], target))
         at += out_rows
     at -= out_rows
-    copies.append((out_down.at[own_out, :], shares.at[at : at + out_rows, taken : taken + LANES]))
-    started = [
-        pltpu.make_async_copy(source, target, sem.at[number])
-        for number, (source, target) in enumerate(copies)
-    ]
-    for copy in started:
-        copy.start()
-    for copy in started:
-        copy.wait()
-
-
-def share_rows(n_exp, heads_wide):
-    return (D // n_exp, LANES // n_exp, heads_wide // n_exp)
-
-
-def pack(place, w_gate, w_up, w_down, w_qkv, qkv_up, w_out, out_down, n_exp):
-    count, _, width = w_gate.shape
+    pairs.append((out_down.at[own_out, :], held.at[at : at + out_rows, taken : taken + LANES]))
+    held[at : at + out_rows, taken + LANES :] = jnp.zeros(
+        (out_rows, wide - taken - LANES), BF16
+    )
+    run_copies(pairs, sem)
+    run_copies([(held, packed)], out_sem)
+
+
+def pack_share(place, w_qkv, qkv_up, w_out, out_down, n_exp):
     qkv_rows, up_rows, out_rows = share_rows(n_exp, w_out.shape[0])
     wide = w_qkv.shape[1]
     pieces = -(-D // wide)
-    copies = count * (2 + D // LANES) + 3 + pieces
+    packed = shape((qkv_rows + up_rows + pieces * out_rows, wide), BF16)
     return pl.pallas_call(
-        functools.partial(pack_kernel, n_exp),
-        in_specs=[IN_SMEM] + [IN_HBM] * 7,
-        out_specs=[IN_HBM] * 2,
-        out_shape=[
-            shape((count, D, 3 * width), BF16),
-            shape((qkv_rows + up_rows + pieces * out_rows, wide), BF16),
+        functools.partial(pack_share_kernel, n_exp),
+        in_specs=[IN_SMEM] + [IN_HBM] * 4,
+        out_specs=IN_HBM,
+        out_shape=packed,
+        scratch_shapes=[
+            pltpu.VMEM(packed.shape, BF16),
+            pltpu.SemaphoreType.DMA((3 + pieces,)),
+            pltpu.SemaphoreType.DMA((1,)),
         ],
-        scratch_shapes=[pltpu.SemaphoreType.DMA((copies,))],
-        name="pack_weights",
-    )(place, w_gate, w_up, w_down, w_qkv, qkv_up, w_out, out_down)
-
-
-def forward_kernel(
-    length_ref, index_ref, tokens_hbm, gain_hbm, w_qkv_hbm, qkv_down_hbm, qkv_up_hbm, w_out_hbm,
-    out_down_hbm, cosine_hbm, sine_hbm,
-    attn_in_ref, low_q_ref, head_ref, base_ref, low_ref,
-    tokens_s, gain_s, w_qkv_s, qkv_down_s, qkv_up_s, w_out_s, out_down_s, cosine_s, sine_s,
-    q_s, k_s, v_s, sem,
-):
-    sources = (
-        tokens_hbm, gain_hbm, qkv_down_hbm, w_qkv_hbm, qkv_up_hbm, cosine_hbm, sine_hbm,
-        w_out_hbm, out_down_hbm,
-    )
-    targets = (
-        tokens_s, gain_s, qkv_down_s, w_qkv_s, qkv_up_s, cosine_s, sine_s, w_out_s, out_down_s,
-    )
-    copies = [
-        pltpu.make_async_copy(source, target, sem.at[number])
-        for number, (source, target) in enumerate(zip(sources, targets))
+        compiler_params=WHOLE_VMEM,
+        cost_estimate=cost(0, 4 * packed.shape[0] * wide),
+        name="pack_share",
+    )(place, w_qkv, qkv_up, w_out, out_down)
+
+
+class Loads:
+    def __init__(self, names, sources, targets, sem):
+        self.copies = {
+            name: pltpu.make_async_copy(source, target, sem.at[number])
+            for number, (name, source, target) in enumerate(zip(names, sources, targets))
+        }
+        self.targets = dict(zip(names, targets))
+        for copy in self.copies.values():
+            copy.start()
+
+    def __getitem__(self, name):
+        copy = self.copies.pop(name, None)
+        if copy is not None:
+            copy.wait()
+        return self.targets[name]
+
+
+def load_scratch(arrays):
+    return [pltpu.VMEM(array.shape, array.dtype) for array in arrays] + [
+        pltpu.SemaphoreType.DMA((len(arrays),))
     ]
-    for copy in copies:
-        copy.start()
-    rows = tokens_s.shape[0]
+
+
+FORWARD_LOADS = (
+    "tokens", "gain", "qkv_down", "w_qkv", "qkv_up", "cosine", "sine", "w_out", "out_down",
+)
+
+
+def forward_kernel(length_ref, index_ref, *refs):
+    count = len(FORWARD_LOADS)
+    attn_in_ref, low_q_ref, head_ref, base_ref, low_ref = refs[count : count + 5]
+    load_sem, q_s, k_s, v_s = refs[2 * count + 5 :]
+    loads = Loads(FORWARD_LOADS, refs[:count], refs[count + 5 : 2 * count + 5], load_sem)
+    rows = attn_in_ref.shape[0]
     groups = k_s.shape[0]
     mask = adapter_mask(length_ref, index_ref, rows, LANES)
     first = first_keys(length_ref, rows)
-    copies[0].wait()
-    copies[1].wait()
-    inputs = tokens_s[...].astype(F32)
+    inputs = loads["tokens"][...].astype(F32)
     inv_root = lax.rsqrt(jnp.mean(inputs * inputs, axis=1, keepdims=True) + EPS)
-    attn_in_ref[...] = (inputs * inv_root * gain_s[...]).astype(BF16)
+    attn_in_ref[...] = (inputs * inv_root * loads["gain"][...]).astype(BF16)
     attn_in = attn_in_ref[...]
-    copies[2].wait()
-    low_q = (dot(attn_in, qkv_down_s[...]) * mask).astype(BF16)
+    low_q = (dot(attn_in, loads["qkv_down"][...]) * mask).astype(BF16)
     low_q_ref[...] = low_q
-    for copy in copies[3:7]:
-        copy.wait()
-    projected = dot(attn_in, w_qkv_s[...]) + dot(low_q, qkv_up_s[...])
-    columns = turn(projected, cosine_s[...], sine_s[...], turned_pieces(groups))
-    store_heads(columns, 0, q_s, k_s, v_s)
+    projected = dot(attn_in, loads["w_qkv"][...]) + dot(low_q, loads["qkv_up"][...])
+    cosine, sine = loads["cosine"][...], loads["sine"][...]
+    store_heads(turn(projected, cosine, sine, turned_pieces(groups)), 0, q_s, k_s, v_s)
     for block in range(rows // ROWS):
         here = slice(block * ROWS, (block + 1) * ROWS)
         keys = (block + 1) * ROWS
@@ -243,19 +290,16 @@
             out = dot(probs, v_s[group, :keys, :])
             heads += [out[head * ROWS : (head + 1) * ROWS] for head in range(PER)]
         head_ref[here, :] = jnp.concatenate(heads, axis=1).astype(BF16)
-    copies[7].wait()
-    copies[8].wait()
     head_out = head_ref[...]
-    base_ref[...] = dot(head_out, w_out_s[...]).astype(BF16)
-    low_ref[...] = (dot(head_out, out_down_s[...]) * mask).astype(BF16)
+    base_ref[...] = dot(head_out, loads["w_out"][...]).astype(BF16)
+    low_ref[...] = (dot(head_out, loads["out_down"][...]) * mask).astype(BF16)
 
 
 def forward(lengths, index, tokens, gain, w_qkv, qkv_down, qkv_up, w_out, out_down, tables):
     rows = tokens.shape[0]
     heads_wide = w_out.shape[0]
     groups = w_qkv.shape[1] // (HD * (PER + 2))
-    blocks = rows // ROWS
-    arrays = (tokens, gain.reshape(1, D), w_qkv, qkv_down, qkv_up, w_out, out_down) + tables
+    arrays = (tokens, gain.reshape(1, D), qkv_down, w_qkv, qkv_up) + tables + (w_out, out_down)
     return pl.pallas_call(
         forward_kernel,
         in_specs=[IN_SMEM] * 2 + [IN_HBM] * len(arrays),
@@ -267,14 +311,14 @@
             shape((rows, D), BF16),
             shape((rows, LANES), BF16),
         ],
-        scratch_shapes=[pltpu.VMEM(array.shape, array.dtype) for array in arrays]
+        scratch_shapes=load_scratch(arrays)
         + [
-            pltpu.VMEM((groups, blocks, PER * ROWS, HD), BF16),
+            pltpu.VMEM((groups, rows // ROWS, PER * ROWS, HD), BF16),
             pltpu.VMEM((groups, rows, HD), BF16),
             pltpu.VMEM((groups, rows, HD), BF16),
-            pltpu.SemaphoreType.DMA((len(arrays),)),
         ],
-        compiler_params=pltpu.CompilerParams(vmem_limit_bytes=48 * MIB),
+        compiler_params=WHOLE_VMEM,
+        cost_estimate=cost(6e9, 10e6),
         name="attention_forward",
     )(lengths, index, *arrays)
 
@@ -377,7 +421,8 @@
             pltpu.VMEM((rows, D), F32),
             pltpu.VMEM((rows, D), F32),
         ],
-        compiler_params=pltpu.CompilerParams(vmem_limit_bytes=60 * MIB),
+        compiler_params=WHOLE_VMEM,
+        cost_estimate=cost(25e9, 30e6),
         name="experts",
     )(*arrays, weights)
 
@@ -389,17 +434,21 @@
     return inv_root * weighted - vectors * (inv_root * inv_root * inv_root) * slope
 
 
-def branch_kernel(
-    length_ref, index_ref, residual_ref, low_o_ref, normed_grad_ref, cot_ref, gain_ref, out_up_ref,
-    head_ref, shares, residual_grad_ref, head_grad_ref, part_ref, w_out_s, sem,
-):
+BRANCH_LOADS = ("residual", "normed_grad", "gain", "cot", "out_up", "low_o", "head")
+
+
+def branch_kernel(length_ref, index_ref, shares, *refs):
+    count = len(BRANCH_LOADS)
+    residual_grad_ref, head_grad_ref, part_ref = refs[count : count + 3]
+    load_sem, w_out_s, sem = refs[2 * count + 3 :]
+    loads = Loads(BRANCH_LOADS, refs[:count], refs[count + 3 : 2 * count + 3], load_sem)
     n_exp, n_tp, _, wide = shares.shape
-    rows = residual_ref.shape[0]
-    qkv_rows, up_rows, out_rows = share_rows(n_exp, w_out_s.shape[1])
+    rows = residual_grad_ref.shape[0]
+    out_rows = w_out_s.shape[1] // n_exp
     copies = []
     for z in range(n_tp):
         for e in range(n_exp):
-            at = qkv_rows + up_rows
+            at = 0
             for left in range(0, D, wide):
                 taken = min(wide, D + LANES - left)
                 copies.append(
@@ -413,16 +462,17 @@
     for copy in copies:
         copy.start()
     mask = adapter_mask(length_ref, index_ref, rows, LANES)
-    low_o = low_o_ref[...]
-    residual_grad_ref[...] = cot_ref[...].astype(F32) + norm_back(
-        residual_ref[...], gain_ref[...], normed_grad_ref[...].astype(F32)
+    residual, normed_grad = loads["residual"][...], loads["normed_grad"][...].astype(F32)
+    residual_grad_ref[...] = loads["cot"][...].astype(F32) + norm_back(
+        residual, loads["gain"][...], normed_grad
     )
     branch_grad = residual_grad_ref[...].astype(BF16)
-    low_o_grad = (dot_nt(branch_grad, out_up_ref[...]) * mask).astype(BF16)
+    low_o_grad = (dot_nt(branch_grad, loads["out_up"][...]) * mask).astype(BF16)
+    low_o = loads["low_o"][...]
     for at in range(D // LANES):
         lanes = slice(at * LANES, (at + 1) * LANES)
         part_ref[lanes, :] = dot_tn(low_o, branch_grad[:, lanes]).astype(BF16)
-    part_ref[D:, :] = dot_tn(head_ref[...], low_o_grad).astype(BF16)
+    part_ref[D:, :] = dot_tn(loads["head"][...], low_o_grad).astype(BF16)
     for copy in copies:
         copy.wait()
     for z in range(n_tp):
@@ -434,34 +484,40 @@
 def branch_back(lengths, index, residual, low_o, normed_grad, cot, gain, out_up, head, shares):
     rows, heads_wide = head.shape
     n_exp, n_tp, _, wide = shares.shape
+    arrays = (residual, normed_grad, gain.reshape(1, D), cot, out_up, low_o, head)
     return pl.pallas_call(
         branch_kernel,
-        in_specs=[IN_SMEM] * 2 + [IN_VMEM] * 7 + [IN_HBM],
+        in_specs=[IN_SMEM] * 2 + [IN_HBM] * (1 + len(arrays)),
         out_specs=[IN_VMEM] * 3,
         out_shape=[
             shape((rows, D), F32),
             shape((n_tp, rows, heads_wide), BF16),
             shape((D + heads_wide, LANES), BF16),
         ],
-        scratch_shapes=[
+        scratch_shapes=load_scratch(arrays)
+        + [
             pltpu.VMEM((n_tp, heads_wide, D + LANES), BF16),
             pltpu.SemaphoreType.DMA((n_tp * n_exp * -(-D // wide),)),
         ],
-        compiler_params=pltpu.CompilerParams(vmem_limit_bytes=48 * MIB),
+        compiler_params=WHOLE_VMEM,
+        cost_estimate=cost(5e9, 20e6),
         name="branch_backward",
-    )(
-        lengths, index, residual, low_o, normed_grad, cot, gain.reshape(1, D), out_up, head, shares
-    )
-
-
-def backward_kernel(
-    place_ref, length_ref, index_ref, attn_in_ref, low_q_ref, head_grad_ref, residual_grad_ref,
-    tokens_ref, gain_ref, qkv_down_ref, cosine_ref, sine_ref, shares,
-    input_grad_ref, part_ref,
-    w_qkv_s, q_s, k_s, v_s, g_s, grad_s, sum_s, sem,
-):
+    )(lengths, index, shares, *arrays)
+
+
+BACKWARD_LOADS = (
+    "attn_in", "low_q", "cosine", "sine", "head_grad", "residual_grad", "tokens", "gain",
+    "qkv_down",
+)
+
+
+def backward_kernel(place_ref, length_ref, index_ref, shares, *refs):
+    count = len(BACKWARD_LOADS)
+    input_grad_ref, part_ref = refs[count : count + 2]
+    load_sem, w_qkv_s, q_s, k_s, v_s, g_s, grad_s, sum_s, sem = refs[2 * count + 2 :]
+    loads = Loads(BACKWARD_LOADS, refs[:count], refs[count + 2 : 2 * count + 2], load_sem)
     n_exp, n_tp, _, wide = shares.shape
-    rows = tokens_ref.shape[0]
+    rows = input_grad_ref.shape[0]
     blocks = rows // ROWS
     groups = k_s.shape[0] // n_tp
     flags = turned_pieces(groups)
@@ -483,18 +539,20 @@
     for copy in copies:
         copy.start()
     first = first_keys(length_ref, rows)
-    attn_in = attn_in_ref[...]
-    low_q = low_q_ref[...]
+    attn_in = loads["attn_in"][...]
+    low_q = loads["low_q"][...]
+    cosine, sine = loads["cosine"], loads["sine"]
+    head_grad = loads["head_grad"]
     seen = [seen_block(first, block) for block in range(blocks)]
     for z in range(n_tp):
         for copy in copies[z * 2 * n_exp : (z + 1) * 2 * n_exp]:
             copy.wait()
         projected = dot(attn_in, w_qkv_s[z, :D, :]) + dot(low_q, w_qkv_s[z, D:, :])
-        columns = turn(projected, cosine_ref[...], sine_ref[...], flags)
+        columns = turn(projected, cosine[...], sine[...], flags)
         store_heads(columns, z * groups, q_s, k_s, v_s)
         for head in range(groups * PER):
             group, kind = divmod(head, PER)
-            part = head_grad_ref[z, :, head * HD : (head + 1) * HD]
+            part = head_grad[z, :, head * HD : (head + 1) * HD]
             for block in range(blocks):
                 g_s[z * groups + group, block, kind * ROWS : (kind + 1) * ROWS, :] = part[
                     block * ROWS : (block + 1) * ROWS
@@ -531,7 +589,7 @@
                 pieces.append(jnp.concatenate([part[here] for part in query_grads], axis=0))
             pieces += [key_grad.T, value_grad.T]
         joined = jnp.concatenate(pieces, axis=1)
-        columns = turn(joined, cosine_ref[...], -sine_ref[...], flags)
+        columns = turn(joined, cosine[...], -sine[...], flags)
         for at, column in enumerate(columns):
             grad_s[z, :, at * LANES : (at + 1) * LANES] = column.astype(BF16)
         return carried
@@ -549,11 +607,10 @@
         part_ref[D + at * LANES : D + (at + 1) * LANES, :] = dot_tn(low_q, own[:, lanes]).astype(
             BF16
         )
-    attn_grad = sum_s[:, :D] + dot_nt(low_q_grad, qkv_down_ref[...])
-    input_grad_ref[...] = (
-        residual_grad_ref[...]
-        + norm_back(tokens_ref[...].astype(F32), gain_ref[...], attn_grad)
-    ).astype(BF16)
+    attn_grad = sum_s[:, :D] + dot_nt(low_q_grad, loads["qkv_down"][...])
+    tokens, gain = loads["tokens"][...].astype(F32), loads["gain"][...]
+    residual_grad = loads["residual_grad"][...]
+    input_grad_ref[...] = (residual_grad + norm_back(tokens, gain, attn_grad)).astype(BF16)
 
 
 def attention_back(
@@ -564,13 +621,15 @@
     n_exp, n_tp, _, wide = shares.shape
     count = KV_HEADS
     blocks = rows // ROWS
-    arrays = (attn_in, low_q, head_grad, residual_grad, tokens, gain.reshape(1, D), qkv_down)
+    arrays = (attn_in, low_q) + tables
+    arrays += (head_grad, residual_grad, tokens, gain.reshape(1, D), qkv_down)
     return pl.pallas_call(
         backward_kernel,
-        in_specs=[IN_SMEM] * 3 + [IN_VMEM] * 9 + [IN_HBM],
+        in_specs=[IN_SMEM] * 3 + [IN_HBM] * (1 + len(arrays)),
         out_specs=[IN_VMEM] * 2,
         out_shape=[shape((rows, D), BF16), shape((D + wide, LANES), BF16)],
-        scratch_shapes=[
+        scratch_shapes=load_scratch(arrays)
+        + [
             pltpu.VMEM((n_tp, D + LANES, wide), BF16),
             pltpu.VMEM((count, blocks, PER * ROWS, HD), BF16),
             pltpu.VMEM((count, rows, HD), BF16),
@@ -580,9 +639,10 @@
             pltpu.VMEM((rows, D + LANES), F32),
             pltpu.SemaphoreType.DMA((n_tp * n_exp * 2,)),
         ],
-        compiler_params=pltpu.CompilerParams(vmem_limit_bytes=60 * MIB),
+        compiler_params=WHOLE_VMEM,
+        cost_estimate=cost(35e9, 20e6),
         name="attention_backward",
-    )(place, lengths, index, *arrays, *tables, shares)
+    )(place, lengths, index, shares, *arrays)
 
 
 def kernel_body(
@@ -591,58 +651,64 @@
 ):
     n_exp = lax.axis_size("exp")
     rows = tokens.shape[0]
-    heads_wide = w_out.shape[0]
-    wide = w_qkv.shape[1]
     exp_place = lax.axis_index("exp").astype(jnp.int32).reshape(1)
     tp_place = lax.axis_index("tp").astype(jnp.int32).reshape(1)
     tables = turn_tables(rows)
-    own_experts, own_shares = pack(
-        exp_place, w_gate, w_up, w_down, w_qkv, qkv_up, w_out, out_down, n_exp
-    )
+    own_experts = pack_experts(w_gate, w_up, w_down)
     weights = lax.all_gather(own_experts, "exp", axis=0, tiled=True)
+    inputs, _ = lax.optimization_barrier((tokens, own_experts))
     attn_in, low_q, head, base, low_o = forward(
-        lengths, adapter_index, tokens, attn_gain, w_qkv, qkv_down, qkv_up, w_out, out_down, tables
-    )
+        lengths, adapter_index, inputs, attn_gain, w_qkv, qkv_down, qkv_up, w_out, out_down, tables
+    )
+    own_share = pack_share(exp_place, w_qkv, qkv_up, w_out, out_down, n_exp)
+    z_shares = lax.all_gather(own_share, "tp", axis=0)
+    base, low_o, _ = lax.optimization_barrier((base, low_o, z_shares))
     base, low_o = lax.psum((base, low_o), "tp")
-    own_shares, _ = lax.optimization_barrier((own_shares, base))
-    shares = lax.all_gather(own_shares, "tp", axis=0)
-    shares, _ = lax.optimization_barrier((shares, weights))
-    shares = lax.all_gather(shares, "exp", axis=0)
+    split = sum(share_rows(n_exp, 0))
+    out_share, _ = lax.optimization_barrier((z_shares[:, split:], weights))
+    out_shares = lax.all_gather(out_share, "exp", axis=0)
     occupied = jnp.arange(rows, dtype=jnp.int32) < jnp.sum(lengths)
     kept = occupied & (loss_mask > 0)
     cot = jnp.where(kept[:, None], upstream, jnp.zeros((), BF16))
     residual, moe_part, normed_part = experts_both(
         tokens, base, low_o, out_up, moe_gain, w_router, routes, cot, weights
     )
+    normed_part, _ = lax.optimization_barrier((normed_part, out_shares))
     normed_grad = lax.psum(normed_part, "tp")
+    qkv_share, _ = lax.optimization_barrier((z_shares[:, :split], normed_part))
+    qkv_shares = lax.all_gather(qkv_share, "exp", axis=0)
     moe_part, _ = lax.optimization_barrier((moe_part, normed_grad))
-    moe_out = lax.psum(moe_part, "tp").astype(F32)
-    output = (residual + moe_out).astype(BF16)
+    moe_out = lax.psum(moe_part, "tp")
+    normed_grad, _ = lax.optimization_barrier((normed_grad, qkv_shares))
     residual_grad, head_grad, out_part = branch_back(
-        lengths, adapter_index, residual, low_o, normed_grad, cot, moe_gain, out_up, head, shares
-    )
+        lengths, adapter_index, residual, low_o, normed_grad, cot, moe_gain, out_up, head,
+        out_shares,
+    )
+    out_parts = lax.all_gather(out_part, "exp", axis=0)
     input_grad, qkv_part = attention_back(
         tp_place, lengths, adapter_index, attn_in, low_q, head_grad, residual_grad, tokens,
-        attn_gain, qkv_down, tables, shares,
-    )
-    parts = jnp.concatenate([out_part, qkv_part], axis=0)
-    share = parts.shape[0] // n_exp
-    parts = lax.all_to_all(parts.reshape(n_exp, share, LANES), "exp", 0, 0, tiled=True)
-    summed = jnp.sum(parts.astype(F32), axis=0).astype(BF16)
-    summed = lax.all_gather(summed, "exp", axis=0, tiled=True).astype(F32)
+        attn_gain, qkv_down, tables, qkv_shares,
+    )
+    moe_out, out_parts, _ = lax.optimization_barrier((moe_out, out_parts, qkv_part))
+    output = (residual + moe_out.astype(F32)).astype(BF16)
+    out_sum = jnp.sum(out_parts.astype(F32), axis=0)
+    share = qkv_part.shape[0] // n_exp
+    parts = lax.all_to_all(qkv_part.reshape(n_exp, share, LANES), "exp", 0, 0, tiled=True)
+    qkv_sum = jnp.sum(parts.astype(F32), axis=0).astype(BF16)
+    spread = jnp.broadcast_to(qkv_sum[None], (n_exp, share, LANES))
+    qkv_sum = lax.all_to_all(spread, "exp", 0, 0, tiled=True).astype(F32).reshape(-1, LANES)
 
     def side_by_side(stacked):
         pieces = stacked.reshape(-1, LANES, LANES)
         return pieces.transpose(1, 0, 2).reshape(LANES, -1)
 
-    at = D + heads_wide
     return (
         output,
         input_grad,
-        summed[at : at + D],
-        side_by_side(summed[at + D :]),
-        summed[D:at],
-        side_by_side(summed[:D]),
+        qkv_sum[:D],
+        side_by_side(qkv_sum[D:]),
+        out_sum[D:],
+        side_by_side(out_sum[:D]),
     )
 
 

time: 469 us -> 544 us (1.16)
  waiting for transfers between devices: 208 us -> 351 us
  Pallas kernels: 188 us -> 116 us
  blocking collectives: 18.7 us -> 28.8 us
    pallas_call x3 -> x4, Pallas kernels: 146 us -> 70.8 us  [the longest x1 50.7 us: attention_back(): pl.pallas_call(backward_kernel, in_specs=[IN_SMEM] * 3 + [IN_HBM] * (1 +...]
    psum x1, waiting for transfers between devices: 0.02 us -> 69.5 us  [kernel_body(): base, low_o = lax.psum((base, low_o), 'tp')]
    all_gather x3 -> x4, waiting for transfers between devices: 52.3 us -> 113 us  [the longest x1 55.5 us: kernel_body(): qkv_shares = lax.all_gather(qkv_share, 'exp', axis=0)]
    psum x1, waiting for transfers between devices: 59.7 us -> 71.3 us  [kernel_body(): normed_grad = lax.psum(normed_part, 'tp')]
    unnamed x60 -> x22, local copies, waits for them, and re-layouts: 16.8 us -> 6.31 us
    all_to_all x1 -> x2, blocking collectives: 18.7 us -> 28.8 us  [the longest x1 15.3 us: kernel_body(): lax.all_to_all(spread, 'exp', 0, 0, tiled=True).astype(F32)]
  transfers between devices with their start and end apart: 7 -> 8, of which waited for: 5 -> 7; matrix products, arithmetic and copies ran while one was open for 2% -> 2% of each run, Pallas kernels for 38% -> 21%
where the time goes in v3:
time: 544 us; the launch traced here: 536 us
  waiting for transfers between devices  351 us (65%)
  Pallas kernels  116 us (21%)
  blocking collectives  28.8 us (5%)
  local copies, waits for them, and re-layouts  16 us (3%)
  between operations  14.7 us (3%)
  other arithmetic  8.49 us (2%)
    all_gather x1, waiting for transfers between devices, kernel_body(): weights = lax.all_gather(own_experts, 'exp', axis=0, tiled=True)  97.2 us
    psum x1, waiting for transfers between devices, kernel_body(): normed_grad = lax.psum(normed_part, 'tp')  71.3 us
    psum x1, waiting for transfers between devices, kernel_body(): base, low_o = lax.psum((base, low_o), 'tp')  69.5 us
    all_gather x1, waiting for transfers between devices, kernel_body(): qkv_shares = lax.all_gather(qkv_share, 'exp', axis=0)  55.5 us
    pallas_call x1, Pallas kernels, attention_back(): pl.pallas_call(backward_kernel, in_specs=[IN_SMEM] * 3 + [IN_HBM] * (1 +...  50.7 us
    pallas_call x1, Pallas kernels, experts_both(): pl.pallas_call(functools.partial(experts_kernel, count), grid=(experts //...  30.5 us
    all_gather x1, waiting for transfers between devices, kernel_body(): z_shares = lax.all_gather(own_share, 'tp', axis=0)  25.1 us
    all_gather x1, waiting for transfers between devices, kernel_body(): out_parts = lax.all_gather(out_part, 'exp', axis=0)  17.1 us
  transfers between devices with their start and end apart: 8, of which 7 were waited for; matrix products, arithmetic and copies ran while one was open for 2% of the time, Pallas kernels for 21%

profile of v3, /device:TPU:0, one launch (start us, length us, event | category | flops | bytes accessed | tf_op | source)
XLA Modules:
  0.0 536.5 jit_solution(15209974218377578352)
XLA Ops:
  7.2 0.0 all-gather.12.cloned.1.call-start
  7.2 1.8 pack_share.1
  9.0 0.0 all-gather.12.cloned.1.call-update
  9.1 0.0 all-gather.10.cloned.1.call-start
  9.1 3.2 pack_experts.1
  12.3 0.0 copy-start.5
  12.3 0.0 all-gather.10.cloned.1.call-update
  12.4 0.0 all-reduce.9.cloned.1.call-start
  12.4 0.6 copy-done.5
  13.0 0.6 reshape.49.refs_1_.refs_7_
  13.6 15.0 %attention_forward.1 = (bf16[512,1536]{1,0:T(8,128)(2,1)}, bf16[512,128]{1,0:T(8,128)(2,1)}, bf16[512,384]{1,0:T(8,128)(2,1)}, bf16[512,1536]{1,0:T(8,128)(2,1)}, bf16[512,128]{1,0:T(8,128)(2,1)}) custom-call(s32[1,4]{1,0:T(1,128)} %length_ref.5, s32[1,4]{1,0:T(1,128)} %index_ref.5, bf16[512,1536]{1,0:T(8,128)(2,1)} %refs_6_.2, ...), custom_call_target="tpu_custom_call" | custom-call | flops 6000000000 | bytes 10000000 | tf_op jit(solution)/shard_map/attention_forward/pallas_call | solution.py:303
  28.6 25.1 %all-gather.12.cloned.1.call-done = bf16[1408,640]{1,0:T(8,128)(2,1)} async-done(((bf16[352,640]{1,0:T(8,128)(2,1)}), bf16[1408,640]{1,0:T(8,128)(2,1)}) %all-gather.12.cloned.1.call-update) | async-done | bytes 1802256 | tf_op jit(solution)/shard_map/all_gather | solution.py:664
  53.7 0.0 all-reduce.9.cloned.1.call-update
  53.8 0.0 copy-start.4
  53.8 0.0 copy-start.7
  53.8 0.0 copy-start.2
  53.8 0.0 all-gather.14.cloned.1.call-start
  53.8 2.2 slice.24
  56.0 97.2 %all-gather.10.cloned.1.call-done.weight_ref = bf16[16,1536,384]{2,1,0:T(8,128)(2,1)} async-done(((bf16[2,1536,384]{2,1,0:T(8,128)(2,1)}), bf16[16,1536,384]{2,1,0:T(8,128)(2,1)}) %all-gather.10.cloned.1.call-update) | async-done | bytes 18874384 | tf_op jit(solution)/shard_map/all_gather | solution.py:658
  153.2 0.0 all-gather.14.cloned.1.call-update
  153.3 0.5 all-reduce.5.cloned.1.call-start
  153.8 0.0 copy-done.8
  153.8 0.6 reduce_sum.30
  154.4 0.0 copy-done.6
  154.4 0.6 reshape.51.gain_ref.refs_2_
  155.0 0.0 copy-done.3
  155.0 0.9 copy.40.router_ref
  156.0 0.0 copy-done.4
  156.0 0.8 copy.41.routes_ref
  156.8 0.0 copy-done.7
  156.8 0.6 fusion
  157.4 1.3 broadcast_select_fusion.cot_ref.refs_3_
  158.8 0.7 copy-done.1
  159.5 1.1 slice.25
  160.6 69.5 %all-reduce.9.cloned.1.call-done = (bf16[512,1536]{1,0:T(8,128)(2,1)}, bf16[512,128]{1,0:T(8,128)(2,1)}) async-done(((bf16[512,1536]{1,0:T(8,128)(2,1)}, bf16[512,128]{1,0:T(8,128)(2,1)}), (bf16[512,1536]{1,0:T(8,128)(2,1)}, bf16[512,128]{1,0:T(8,128)(2,1)})) %all-reduce.9.cloned.1.call-update) | async-done | bytes 1703952 | tf_op jit(solution)/shard_map/psum | solution.py:666
  230.0 30.5 %experts.1 = (f32[512,1536]{1,0:T(8,128)}, bf16[512,1536]{1,0:T(8,128)(2,1)}, bf16[512,1536]{1,0:T(8,128)(2,1)}) custom-call(bf16[512,1536]{1,0:T(8,128)(2,1)} %refs_6_.2, bf16[512,1536]{1,0:T(8,128)(2,1)} %get-tuple-element.70.base_ref, bf16[512,128]{1,0:T(8,128)(2,1)} %get-tuple-element.71.low_o_ref.refs_5_, bf16[128,1536]{1,0:T(8,128)(2,1)} %refs_4_.3, ...), custom_call_target="tpu_custom_call" | custom-call | flops 24999999488 | bytes 30000000 | tf_op jit(solution)/shard_map/experts/pallas_call | solution.py:410
  260.5 14.8 %all-gather.14.cloned.1.call-done = bf16[32,144,640]{2,1,0:T(8,128)(2,1)} async-done(((bf16[4,144,640]{2,1,0:T(8,128)(2,1)}), bf16[32,144,640]{2,1,0:T(8,128)(2,1)}) %all-gather.14.cloned.1.call-update) | async-done | bytes 5898256 | tf_op jit(solution)/shard_map/all_gather | solution.py:669
  275.3 0.0 all-reduce.5.cloned.1.call-update
  275.3 0.0 all-gather.16.cloned.1.call-start
  275.4 0.5 all-gather.16.cloned.1.call-update
  275.9 0.0 all-reduce.7.cloned.1.call-start
  275.9 71.3 %all-reduce.5.cloned.1.call-done.refs_1_ = bf16[512,1536]{1,0:T(8,128)(2,1)} async-done(((bf16[512,1536]{1,0:T(8,128)(2,1)}), bf16[512,1536]{1,0:T(8,128)(2,1)}) %all-reduce.5.cloned.1.call-update) | async-done | bytes 1572880 | tf_op jit(solution)/shard_map/psum | solution.py:677
  347.2 0.0 all-reduce.7.cloned.1.call-update
  347.3 0.2 all-gather.18.cloned.1.call-start
  347.5 55.5 %all-gather.16.cloned.1.call-done = bf16[32,208,640]{2,1,0:T(8,128)(2,1)} async-done(((bf16[4,208,640]{2,1,0:T(8,128)(2,1)}), bf16[32,208,640]{2,1,0:T(8,128)(2,1)}) %all-gather.16.cloned.1.call-update) | async-done | bytes 8519696 | tf_op jit(solution)/shard_map/all_gather | solution.py:679
  403.0 15.1 %branch_backward.1 = (f32[512,1536]{1,0:T(8,128)}, bf16[4,512,384]{2,1,0:T(8,128)(2,1)}, bf16[1920,128]{1,0:T(8,128)(2,1)}) custom-call(s32[1,4]{1,0:T(1,128)} %length_ref.5, s32[1,4]{1,0:T(1,128)} %index_ref.5, bf16[8,4,144,640]{3,2,1,0:T(8,128)(2,1)} %bitcast.27, f32[512,1536]{1,0:T(8,128)} %get-tuple-element.34.refs_0_, ...), custom_call_target="tpu_custom_call" | custom-call | flops 5000000000 | bytes 20000000 | tf_op jit(solution)/shard_map/branch_backward/pallas_call | solution.py:488
  418.2 0.0 all-gather.18.cloned.1.call-update
  418.2 50.7 %attention_backward.1 = (bf16[512,1536]{1,0:T(8,128)(2,1)}, bf16[2176,128]{1,0:T(8,128)(2,1)}) custom-call(s32[1]{0:T(128)} %bitcast.5.place_ref, s32[1,4]{1,0:T(1,128)} %length_ref.5, s32[1,4]{1,0:T(1,128)} %index_ref.5, bf16[8,4,208,640]{3,2,1,0:T(8,128)(2,1)} %bitcast.26, bf16[512,1536]{1,0:T(8,128)(2,1)} %get-tuple-element.44.refs_0_, ...), custom_call_target="tpu_custom_call" | custom-call | flops 35000000512 | bytes 20000000 | tf_op jit(solution)/shard_map/attention_backward/pallas_call | solution.py:626
  468.9 13.5 %all_to_all.10 = bf16[8,272,128]{2,1,0:T(8,128)(2,1)S(1)} all-to-all(bf16[8,272,128]{2,1,0:T(8,128)(2,1)} %bitcast.25), channel_id=1, replica_groups=mesh['exp'=8,'tp'=4] {'exp'}, dimensions={0} | all-to-all | bytes 1114112 | tf_op jit(solution)/shard_map/all_to_all | solution.py:696
  482.4 0.1 reduce_sum.31
  482.5 0.1 broadcast_in_dim.21
  482.6 15.3 %all_to_all.11 = bf16[8,272,128]{2,1,0:T(8,128)(2,1)S(1)} all-to-all(bf16[8,272,128]{2,1,0:T(8,128)(2,1)S(1)} %broadcast_in_dim.21), channel_id=1, replica_groups=mesh['exp'=8,'tp'=4] {'exp'}, dimensions={0} | all-to-all | bytes 1114112 | tf_op jit(solution)/shard_map/all_to_all | solution.py:699
  497.8 0.1 bitcast_convert_fusion
  498.0 0.9 slice.26
  498.9 0.2 copy.42
  499.1 0.9 copy.44
  500.0 17.1 %all-gather.18.cloned.1.call-done = bf16[15360,128]{1,0:T(8,128)(2,1)} async-done(((bf16[1920,128]{1,0:T(8,128)(2,1)}), bf16[15360,128]{1,0:T(8,128)(2,1)}) %all-gather.18.cloned.1.call-update) | async-done | bytes 3932176 | tf_op jit(solution)/shard_map/all_gather | solution.py:687
  517.1 2.7 convert_reduce_fusion
  519.8 0.9 slice.29
  520.8 0.7 slice.28
  521.5 2.4 copy.43
  523.9 2.3 copy.45
  526.2 0.0 copy-done
  526.2 3.0 add_convert_fusion
  (8 shorter events, 0.0 us)
Async XLA Ops:
  7.2 46.6 %all-gather.12.cloned.1.call-start = ((), (), s32[]{:S(2)}) async-start(), calls=%async_computation.5 | async-start | bytes 2252800 | tf_op jit(solution)/shard_map/all_gather | solution.py:664
  9.1 144.2 %all-gather.10.cloned.1.call-start = ((), (), s32[]{:S(2)}) async-start(), calls=%async_computation.2 | async-start | bytes 21233664 | tf_op jit(solution)/shard_map/all_gather | solution.py:658
  12.3 0.7 copy-start.5
  12.4 217.7 %all-reduce.9.cloned.1.call-start = ((), (), s32[]{:S(2)}) async-start(), calls=%async_computation.9 | async-start | bytes 3407872 | tf_op jit(solution)/shard_map/psum | solution.py:666
  53.7 100.1 %copy-start.8 = (s32[1,4]{1,0:T(1,128)S(1)}, s32[1,4]{1,0:T(1,128)}, u32[]{:S(2)}) copy-start(s32[1,4]{1,0:T(1,128)} %length_ref.5) | copy-start | bytes 52
  53.7 100.7 %copy-start.6 = (f32[1536]{0:T(1024)S(1)}, f32[1536]{0:T(1024)}, u32[]{:S(2)}) copy-start(f32[1536]{0:T(1024)} %param.22) | copy-start | bytes 18436
  53.7 101.3 %copy-start.3 = (bf16[1536,16]{0,1:T(8,128)(2,1)S(1)}, bf16[1536,16]{0,1:T(8,128)(2,1)}, u32[]{:S(2)}) copy-start(bf16[1536,16]{0,1:T(8,128)(2,1)} %param.25) | copy-start | bytes 147460
  53.8 102.2 %copy-start.4 = (s32[512,8]{0,1:T(8,128)S(1)}, s32[512,8]{0,1:T(8,128)}, u32[]{:S(2)}) copy-start(s32[512,8]{0,1:T(8,128)} %param.36) | copy-start | bytes 49156
  53.8 103.0 %copy-start.7 = (s32[512]{0:T(512)S(1)}, s32[512]{0:T(512)}, u32[]{:S(2)}) copy-start(s32[512]{0:T(512)} %param.35) | copy-start | bytes 6148
  53.8 103.6 %copy-start.2 = (bf16[512,1536]{1,0:T(8,128)(2,1)S(1)}, bf16[512,1536]{1,0:T(8,128)(2,1)}, u32[]{:S(2)}) copy-start(bf16[512,1536]{1,0:T(8,128)(2,1)} %param.37) | copy-start | bytes 4718596
  53.8 221.5 %all-gather.14.cloned.1.call-start = ((), (), s32[]{:S(2)}) async-start(), calls=%async_computation.6 | async-start | bytes 6635520 | tf_op jit(solution)/shard_map/all_gather | solution.py:669
  153.3 194.0 %all-reduce.5.cloned.1.call-start = ((), (), s32[]{:S(2)}) async-start(), calls=%async_computation.3 | async-start | bytes 3145728 | tf_op jit(solution)/shard_map/psum | solution.py:677
  157.4 2.1 copy-start.1
  275.3 127.7 %all-gather.16.cloned.1.call-start = ((), (), s32[]{:S(2)}) async-start(), calls=%async_computation.7 | async-start | bytes 9584640 | tf_op jit(solution)/shard_map/all_gather | solution.py:679
  275.9 224.1 %all-reduce.7.cloned.1.call-start = ((), (), s32[]{:S(2)}) async-start(), calls=%async_computation.4 | async-start | bytes 3145728 | tf_op jit(solution)/shard_map/psum | solution.py:681
  347.3 169.8 %all-gather.18.cloned.1.call-start = ((), (), s32[]{:S(2)}) async-start(), calls=%async_computation.8 | async-start | bytes 4423680 | tf_op jit(solution)/shard_map/all_gather | solution.py:687
  521.5 4.7 copy-start
Sparse Core Ops, SparseCore 0:
  10.1 43.5 all-gather.11
  55.6 97.5 all-gather.9
  156.3 73.7 all-reduce.8
  232.4 42.8 all-gather.13
  278.1 69.1 all-reduce.4
  349.0 53.9 all-gather.15
  405.4 69.1 all-reduce.6
  476.4 40.6 all-gather.17
